TPU v7x, 32 devices: a whole 2x2x4 slice. The times are simulated.
32 devices in a mesh: dp: 8 (over y, x, core), mp: 4 (over z).
Axes of the slice: x: 2, y: 2, z: 4, core: 2. Of those that a mesh axis runs over, the one named last changes fastest.
Arguments:
- tokens: bfloat16 [12544, 1024], P(('dp', 'mp')), may hold values from -6 to 6
- cotangent: bfloat16 [12544, 1024], P(('dp', 'mp')), may hold values from -6.2 to 6.2
- in_master: float32 [1024, 7168], P('dp', 'mp'), as said below
- in_first: float32 [1024, 7168], P('dp', 'mp')
- in_second: float32 [1024, 7168], P('dp', 'mp'), as said below
- out_master: float32 [1024, 5120], P('dp', 'mp'), as said below
- out_first: float32 [1024, 5120], P('dp', 'mp')
- out_second: float32 [1024, 5120], P('dp', 'mp'), as said below
- gains: float32 [1152], replicated, as said below
- gain_first: float32 [1152], replicated
- gain_second: float32 [1152], replicated, as said below
Outputs:
- block_out: bfloat16 [12544, 1024], P(('dp', 'mp'))
- input_grad: bfloat16 [12544, 1024], P(('dp', 'mp'))
- in_first_new: float32 [1024, 7168], P('dp', 'mp')
- in_second_new: float32 [1024, 7168], P('dp', 'mp')
- in_master_new: float32 [1024, 7168], P('dp', 'mp')
- in_copy: bfloat16 [1024, 7168], P('dp', 'mp')
- out_first_new: float32 [1024, 5120], P('dp', 'mp')
- out_second_new: float32 [1024, 5120], P('dp', 'mp')
- out_master_new: float32 [1024, 5120], P('dp', 'mp')
- out_copy: bfloat16 [1024, 5120], P('dp', 'mp')
- gain_first_new: float32 [1152], replicated
- gain_second_new: float32 [1152], replicated
- gains_new: float32 [1152], replicated
- grad_norm: float32 [], replicated
- norm_table: float32 [5, 2], replicated
Inputs may be any that keep to these rules, and one draw needn't show every extreme that they name: `in_master`: weights of order one over the root of their fan-in. `out_master`: weights of order one over the root of their fan-in. `in_second`: every entry positive. `out_second`: every entry positive. `gains`: every entry positive. `gain_second`: every entry positive.
All inputs are finite; a program needn't handle non-finite values.
Results may differ from a plain program's by a relative error of at most 0.015.
Values may be sent and summed in bfloat16 or wider, within the bound.
No kernel may reach another device: no remote copies, remote signals or barrier semaphores. Data moves between devices by JAX's collectives and lax.ppermute only.
A program may use at most 128 MiB of HBM per device.

v0:
```python
import math

import jax
import jax.numpy as jnp
from jax import lax
from jax.sharding import PartitionSpec as P

D = 1024
DH = 64
PATCHES = 196
STEP = 10
UNITS = 256


norm_eps = 1e-06
lamb_eps = 1e-06
beta_first = 0.5
beta_second = 0.5
rate_step = 0.5
decay_matrix = 0.01


def layer_norm(values, gain):
    centered = values - jnp.mean(values, axis=-1, keepdims=True)
    variance = jnp.mean(centered * centered, axis=-1, keepdims=True)
    return centered * lax.rsqrt(variance + norm_eps) * gain


def project_pieces(joined, q_gain, k_gain):
    row_total = joined.shape[0]
    local_heads = joined.shape[1] // (3 * DH + UNITS)
    parts = joined.reshape(row_total, local_heads, 3 * DH + UNITS)
    query = layer_norm(parts[..., :DH], q_gain)
    keys = layer_norm(parts[..., DH : 2 * DH], k_gain)
    values = parts[..., 2 * DH : 3 * DH]
    activated = jax.nn.gelu(parts[..., 3 * DH :])
    return (query, keys, values, activated)


def per_image(values):
    row_total, local_heads, width = values.shape
    return values.astype(jnp.bfloat16).reshape(row_total // PATCHES, PATCHES, local_heads, width)


def attention_probs(query_img, keys_img):
    scores = jnp.einsum(
        "iphd,iqhd->ihpq", query_img, keys_img, preferred_element_type=jnp.float32
    ) * (1.0 / math.sqrt(DH))
    return jax.nn.softmax(scores, axis=-1)


def mix_block(normed_block, in_weight, q_gain, k_gain):
    joined = jnp.dot(normed_block, in_weight, preferred_element_type=jnp.float32)
    query, keys, values, activated = project_pieces(joined, q_gain, k_gain)
    row_total, local_heads = (query.shape[0], query.shape[1])
    values_img = per_image(values)
    probs = attention_probs(per_image(query), per_image(keys))
    attended = jnp.einsum(
        "ihpq,iqhd->iphd",
        probs.astype(jnp.bfloat16),
        values_img,
        preferred_element_type=jnp.float32,
    ).astype(jnp.bfloat16)
    mixed = jnp.concatenate(
        [attended.reshape(row_total, local_heads, DH), activated.astype(jnp.bfloat16)], axis=-1
    )
    return mixed.reshape(row_total, local_heads * (DH + UNITS))


def back_block(carry, inputs, in_weight, out_weight, q_gain, k_gain):
    in_acc, out_acc, norm_acc = carry
    normed_block, grad_block, mixed_block = inputs
    joined = jnp.dot(normed_block, in_weight, preferred_element_type=jnp.float32)
    (query, keys, values, activated), pull = jax.vjp(project_pieces, joined, q_gain, k_gain)
    row_total, local_heads = (query.shape[0], query.shape[1])
    query_img = per_image(query)
    keys_img = per_image(keys)
    values_img = per_image(values)
    probs = attention_probs(query_img, keys_img)
    mixed_grad = jnp.dot(grad_block, out_weight, preferred_element_type=jnp.float32).reshape(
        row_total, local_heads, DH + UNITS
    )
    attended_grad = per_image(mixed_grad[..., :DH])
    act_grad = mixed_grad[..., DH:]
    probs_grad = jnp.einsum(
        "iphd,iqhd->ihpq", attended_grad, values_img, preferred_element_type=jnp.float32
    )
    score_grad = (
        probs * (probs_grad - jnp.sum(probs * probs_grad, axis=-1, keepdims=True))
    ).astype(jnp.bfloat16)
    scale_factor = 1.0 / math.sqrt(DH)
    query_grad = (
        jnp.einsum("ihpq,iqhd->iphd", score_grad, keys_img, preferred_element_type=jnp.float32)
        * scale_factor
    )
    keys_grad = (
        jnp.einsum("ihpq,iphd->iqhd", score_grad, query_img, preferred_element_type=jnp.float32)
        * scale_factor
    )
    values_grad = jnp.einsum(
        "ihpq,iphd->iqhd",
        probs.astype(jnp.bfloat16),
        attended_grad,
        preferred_element_type=jnp.float32,
    )
    head_shape = (row_total, local_heads, DH)
    joined_grad, q_gain_grad, k_gain_grad = pull(
        (
            query_grad.reshape(head_shape),
            keys_grad.reshape(head_shape),
            values_grad.reshape(head_shape),
            act_grad,
        )
    )
    joined_low = joined_grad.astype(jnp.bfloat16)
    by_rows = (((0,), (0,)), ((), ()))
    in_acc = in_acc + lax.dot_general(
        normed_block, joined_low, by_rows, preferred_element_type=jnp.float32
    )
    out_acc = out_acc + lax.dot_general(
        grad_block, mixed_block, by_rows, preferred_element_type=jnp.float32
    )
    norm_acc = norm_acc + jnp.concatenate([q_gain_grad, k_gain_grad])
    return ((in_acc, out_acc, norm_acc), joined_low)


def moments(grad, first, second, weight, decay):
    first_new = beta_first * first + (1.0 - beta_first) * grad
    second_new = beta_second * second + (1.0 - beta_second) * grad * grad
    first_hat = first_new / (1.0 - beta_first**STEP)
    second_hat = second_new / (1.0 - beta_second**STEP)
    update = first_hat / (jnp.sqrt(second_hat) + lamb_eps) + decay * weight
    return (first_new, second_new, update)


def local_trust(weight, update):
    weight_norm = jnp.sqrt(jnp.sum(weight * weight))
    update_norm = jnp.sqrt(jnp.sum(update * update))
    return (weight_norm, update_norm, weight - rate_step * (weight_norm / update_norm) * update)


def on_device(
    tokens,
    cotangent,
    in_master,
    in_first,
    in_second,
    out_master,
    out_first,
    out_second,
    gains,
    gain_first,
    gain_second,
):
    in_weight, out_weight = (
        lax.all_gather(in_master.astype(jnp.bfloat16), "dp", axis=0, tiled=True),
        lax.all_gather(out_master.astype(jnp.bfloat16), "dp", axis=0, tiled=True),
    )
    shard_count = lax.axis_size("mp")
    row_count = tokens.shape[0]
    ln_gain = gains[:D]
    q_gain = gains[D : D + DH]
    k_gain = gains[D + DH :]
    rows_in = tokens.astype(jnp.float32)
    normed = layer_norm(rows_in, ln_gain).astype(jnp.bfloat16)
    normed_all = lax.all_gather(normed, "mp", axis=0, tiled=True)
    normed_blocks = normed_all.reshape(shard_count, row_count, D)
    mixed_blocks = lax.map(lambda block: mix_block(block, in_weight, q_gain, k_gain), normed_blocks)
    mixed_all = mixed_blocks.reshape(shard_count * row_count, mixed_blocks.shape[2])
    block = mixed_all
    branch = lax.psum_scatter(
        lax.dot_general(
            block, out_weight, (((1,), (1,)), ((), ())), preferred_element_type=jnp.float32
        ).astype(jnp.bfloat16),
        "mp",
        scatter_dimension=0,
        tiled=True,
    ).astype(jnp.float32)
    block_out = (rows_in + branch).astype(jnp.bfloat16)
    grad_all = lax.all_gather(cotangent, "mp", axis=0, tiled=True)
    carry_start = (
        jnp.zeros((D, in_weight.shape[1]), jnp.float32),
        jnp.zeros((D, out_weight.shape[1]), jnp.float32),
        jnp.zeros((2 * DH,), jnp.float32),
    )

    def back_step(carry, inputs):
        return back_block(carry, inputs, in_weight, out_weight, q_gain, k_gain)

    (in_acc, out_acc, norm_acc), joined_blocks = lax.scan(
        back_step,
        carry_start,
        (normed_blocks, grad_all.reshape(shard_count, row_count, D), mixed_blocks),
    )
    joined_all = joined_blocks.reshape(shard_count * row_count, joined_blocks.shape[2])
    block = joined_all
    normed_grad = lax.psum_scatter(
        lax.dot_general(
            block, in_weight, (((1,), (1,)), ((), ())), preferred_element_type=jnp.float32
        ).astype(jnp.bfloat16),
        "mp",
        scatter_dimension=0,
        tiled=True,
    ).astype(jnp.float32)
    unused_value, ln_pull = jax.vjp(layer_norm, rows_in, ln_gain)
    rows_grad, ln_grad = ln_pull(normed_grad)
    input_grad = (cotangent.astype(jnp.float32) + rows_grad).astype(jnp.bfloat16)
    gain_grad = lax.psum(jnp.concatenate([ln_grad, norm_acc]), ("dp", "mp"))
    own_rows = in_master.shape[0]
    in_total, out_total = (
        lax.psum(in_acc.astype(jnp.bfloat16), "dp").astype(jnp.float32),
        lax.psum(out_acc.astype(jnp.bfloat16), "dp").astype(jnp.float32),
    )
    row_start = lax.axis_index("dp") * own_rows
    in_grad = lax.dynamic_slice_in_dim(in_total, row_start, own_rows, 0)
    out_grad = lax.dynamic_slice_in_dim(out_total, row_start, own_rows, 0)
    squares = lax.psum(
        (
            jnp.sum(in_grad * in_grad),
            jnp.sum(out_grad * out_grad),
            jnp.sum(in_master * in_master),
            jnp.sum(out_master * out_master),
        ),
        ("dp", "mp"),
    )
    grad_norm = jnp.sqrt(squares[0] + squares[1] + jnp.sum(gain_grad * gain_grad))
    factor = 1.0 / jnp.maximum(grad_norm, 1.0)
    in_first_new, in_second_new, in_update = moments(
        in_grad * factor, in_first, in_second, in_master, decay_matrix
    )
    out_first_new, out_second_new, out_update = moments(
        out_grad * factor, out_first, out_second, out_master, decay_matrix
    )
    gain_first_new, gain_second_new, gain_update = moments(
        gain_grad * factor, gain_first, gain_second, gains, 0.0
    )
    update_squares = lax.psum(
        (jnp.sum(in_update * in_update), jnp.sum(out_update * out_update)), ("dp", "mp")
    )
    in_wnorm = jnp.sqrt(squares[2])
    in_unorm = jnp.sqrt(update_squares[0])
    out_wnorm = jnp.sqrt(squares[3])
    out_unorm = jnp.sqrt(update_squares[1])
    in_master_new = in_master - rate_step * (in_wnorm / in_unorm) * in_update
    out_master_new = out_master - rate_step * (out_wnorm / out_unorm) * out_update
    ln_wnorm, ln_unorm, ln_new = local_trust(gains[:D], gain_update[:D])
    q_wnorm, q_unorm, q_new = local_trust(gains[D : D + DH], gain_update[D : D + DH])
    k_wnorm, k_unorm, k_new = local_trust(gains[D + DH :], gain_update[D + DH :])
    gains_new = jnp.concatenate([ln_new, q_new, k_new])
    norm_table = jnp.stack(
        [
            jnp.stack([in_wnorm, in_unorm]),
            jnp.stack([out_wnorm, out_unorm]),
            jnp.stack([ln_wnorm, ln_unorm]),
            jnp.stack([q_wnorm, q_unorm]),
            jnp.stack([k_wnorm, k_unorm]),
        ]
    )
    in_copy = in_master_new.astype(jnp.bfloat16)
    out_copy = out_master_new.astype(jnp.bfloat16)
    return (
        block_out,
        input_grad,
        in_first_new,
        in_second_new,
        in_master_new,
        in_copy,
        out_first_new,
        out_second_new,
        out_master_new,
        out_copy,
        gain_first_new,
        gain_second_new,
        gains_new,
        grad_norm,
        norm_table,
    )


def solution(mesh):
    in_specs = (
        P(("dp", "mp"), None),
        P(("dp", "mp"), None),
        P("dp", "mp"),
        P("dp", "mp"),
        P("dp", "mp"),
        P("dp", "mp"),
        P("dp", "mp"),
        P("dp", "mp"),
        P(),
        P(),
        P(),
    )
    out_specs = (
        P(("dp", "mp"), None),
        P(("dp", "mp"), None),
        P("dp", "mp"),
        P("dp", "mp"),
        P("dp", "mp"),
        P("dp", "mp"),
        P("dp", "mp"),
        P("dp", "mp"),
        P("dp", "mp"),
        P("dp", "mp"),
        P(),
        P(),
        P(),
        P(),
        P(),
    )
    return jax.shard_map(
        on_device, mesh=mesh, in_specs=in_specs, out_specs=out_specs, check_vma=False
    )
```

profile of v0, /device:TPU:0, one launch (start us, length us, event | category | flops | bytes accessed | tf_op | source)
XLA Modules:
  0.0 872.9 jit_solution(4745834186306112435)
XLA Ops:
  18.1 63.3 %all-gather.5.cloned.1.call-done = bf16[1568,1024]{1,0:T(8,128)(2,1)} async-done(((bf16[392,1024]{1,0:T(8,128)(2,1)}), bf16[1568,1024]{1,0:T(8,128)(2,1)}) %all-gather.5.cloned.1.call-update) | async-done | bytes 3211280 | tf_op jit(solution)/shard_map/all_gather | solution.py:166
  81.4 36.2 %all-gather.7.cloned.1.call-done = bf16[1024,1792]{0,1:T(8,128)(2,1)} async-done(((bf16[128,1792]{0,1:T(8,128)(2,1)}), bf16[1024,1792]{0,1:T(8,128)(2,1)}) %all-gather.7.cloned.1.call-update) | async-done | bytes 3670032 | tf_op jit(solution)/shard_map/all_gather | solution.py:156
  117.6 106.2 %while.29 = (s32[]{:T(128)}, bf16[4,392,1280]{2,1,0:T(8,128)(2,1)}, bf16[4,392,1024]{2,1,0:T(8,128)(2,1)}, bf16[1024,1792]{0,1:T(8,128)(2,1)}, f32[64]{0:T(128)S(1)}, /*index=5*/f32[64]{0:T(128)S(1)}, s32[]{:T(128)}) while((s32[]{:T(128)}, bf16[4,392,1280]{2,1,0:T(8,128)(2,1)}, bf16[4,392,1024]{2,1,0:T(8,128)(2,1)}, ...), condition=%wide.region_9.10_spmd, body=%wide.region_2.9_spmd.sunk | while | flops 1526187904 | bytes 27128936 | solution.py:168
  117.6 4.1 fusion.163
  129.6 3.0 exponential_reduce_fusion.4
  144.2 4.1 fusion.163
  156.1 3.0 exponential_reduce_fusion.4
  170.7 4.2 fusion.163
  182.7 3.0 exponential_reduce_fusion.4
  197.3 4.1 fusion.163
  209.3 3.0 exponential_reduce_fusion.4
  223.8 351.8 %while.30 = (s32[]{:T(128)}, f32[1024,1792]{1,0:T(8,128)}, f32[1024,1280]{1,0:T(8,128)}, f32[128]{0:T(128)}, bf16[4,392,1792]{2,1,0:T(8,128)(2,1)}, /*index=5*/b...) while((s32[]{:T(128)}, f32[1024,1792]{1,0:T(8,128)}, ...), condition=%wide.region_25.26_spmd.clone, body=%wide.region_11.25_spmd.clone.sunk | while | flops 5195603968 | bytes 120276328 | solution.py:190
  224.0 4.1 fusion.186
  239.1 2.8 exponential_reduce_fusion.5
  244.7 3.4 fusion.189
  270.2 3.5 multiply_reduce_fusion.32
  283.9 3.9 broadcast_add_fusion.3
  292.5 6.2 select_add_fusion.4
  301.7 5.3 select_add_fusion.5
  307.0 4.1 fusion.186
  327.6 3.4 fusion.189
  353.2 3.5 multiply_reduce_fusion.32
  366.9 3.9 broadcast_add_fusion.3
  375.5 8.5 select_add_fusion.4
  386.9 6.9 select_add_fusion.5
  393.8 4.1 fusion.186
  414.4 3.4 fusion.189
  440.0 3.5 multiply_reduce_fusion.32
  453.6 3.9 broadcast_add_fusion.3
  462.3 8.5 select_add_fusion.4
  473.6 6.9 select_add_fusion.5
  480.5 4.1 fusion.186
  495.6 2.8 exponential_reduce_fusion.5
  501.1 3.4 fusion.189
  526.7 3.5 multiply_reduce_fusion.32
  540.4 3.9 broadcast_add_fusion.3
  549.0 8.5 select_add_fusion.4
  560.4 6.9 select_add_fusion.5
  575.6 5.4 convert_element_type.135
  582.9 10.6 %convolution_convert_fusion.1 = bf16[1568,1024]{1,0:T(8,128)(2,1)} fusion(bf16[1568,1792]{1,0:T(8,128)(2,1)} %bitcast.157, bf16[1024,1792]{0,1:T(8,128)(2,1)} %get-tuple-element.644), kind=kOutput, calls=%fused_computation.121 | convolution fusion | flops 5756190720 | bytes 12500992 | tf_op jit(solution)/shard_map/dot_general | solution.py:198
  595.3 8.0 convolution_convert_fusion.2
  604.7 82.8 %all-reduce.9.cloned.1.call-done = (bf16[1024,1792]{1,0:T(8,128)(2,1)}, bf16[1024,1280]{1,0:T(8,128)(2,1)}) async-done(((bf16[1024,1792]{1,0:T(8,128)(2,1)}, bf16[1024,1280]{1,0:T(8,128)(2,1)}), (bf16[1024,1792]{1,0:T(8,128)(2,1)}, bf16[1024,1280]{1,0:T(8,128)(2,1)})) %all-reduce.9.cloned.1.call-update) | async-done | bytes 6291472 | tf_op jit(solution)/shard_map/psum | solution.py:211
  692.5 58.8 %reduce-scatter.5.cloned.1.call-done = bf16[392,1024]{1,0:T(8,128)(2,1)} async-done(((bf16[1568,1024]{1,0:T(8,128)(2,1)}), bf16[392,1024]{1,0:T(8,128)(2,1)}) %reduce-scatter.5.cloned.1.call-update) | async-done | bytes 802832 | tf_op jit(solution)/shard_map/reduce_scatter | solution.py:197
  754.6 44.1 %all-reduce.5 = (f32[]{:T(128)}, f32[1152]{0:T(1024)S(1)}) all-reduce(f32[]{:T(128)S(6)} %add.200, f32[1152]{0:T(1024)S(1)} %pad_maximum_fusion.1), channel_id=1, replica_groups=mesh['dp'=8,'mp'=4] {'dp','mp'}, use_global_device_ids=true, to_apply=%region_31.32 | all-reduce | flops 1153 | bytes 9224 | tf_op jit(solution)/shard_map/psum | solution.py:217
  800.8 3.7 multiply_reduce_fusion.13
  804.5 3.6 multiply_reduce_fusion.11
  808.2 40.1 %all-reduce.4 = (f32[]{:T(128)}, f32[]{:T(128)}, f32[]{:T(128)}, f32[]{:T(128)}) all-reduce(f32[]{:T(128)} %get-tuple-element.289, f32[]{:T(128)} %get-tuple-element.288, f32[]{:T(128)} %get-tuple-element.291, f32[]{:T(128)} %get-tuple-element.290), channel_id=1, replica_groups=mesh['dp'=8,'mp'=4] {'dp','mp'}, use_global_device_ids=true, to_apply=%region_39.40 | all-reduce | flops 4 | bytes 32 | tf_op jit(solution)/shard_map/psum | solution.py:217
  861.8 3.0 add_convert_fusion.1
  (413 shorter events, 326.6 us)
Async XLA Ops:
  7.2 5.5 copy-start.9
  7.2 74.2 %all-gather.5.cloned.1.call-start = ((), (), s32[]{:S(2)}) async-start(), calls=%async_computation.2 | async-start | bytes 4014080 | tf_op jit(solution)/shard_map/all_gather | solution.py:166
  8.6 5.3 copy-start.12
  8.6 3.5 copy-start.24
  13.9 103.7 %all-gather.7.cloned.1.call-start = ((), (), s32[]{:S(2)}) async-start(), calls=%async_computation.3 | async-start | bytes 4128768 | tf_op jit(solution)/shard_map/all_gather | solution.py:156
  15.0 208.8 %all-gather.9.cloned.1.call-start = ((), (), s32[]{:S(2)}) async-start(), calls=%async_computation.4 | async-start | bytes 2949120 | tf_op jit(solution)/shard_map/all_gather | solution.py:157
  16.0 207.8 %all-gather.11.cloned.1.call-start = ((), (), s32[]{:S(2)}) async-start(), calls=%async_computation.6 | async-start | bytes 4014080 | tf_op jit(solution)/shard_map/all_gather | solution.py:180
  16.5 671.0 %all-reduce.9.cloned.1.call-start = ((), (), s32[]{:S(2)}) async-start(), calls=%async_computation.8 | async-start | bytes 12582912 | tf_op jit(solution)/shard_map/psum | solution.py:211
  248.1 1.4 copy-start.5
  254.1 2.2 copy-start.7
  262.9 1.8 copy-start.3
  270.2 3.5 copy-start.1
  283.9 3.9 copy-start.6
  331.1 1.4 copy-start.5
  337.0 2.2 copy-start.7
  345.9 1.8 copy-start.3
  353.2 3.5 copy-start.1
  366.9 3.9 copy-start.6
  417.8 1.4 copy-start.5
  423.8 2.2 copy-start.7
  432.7 1.8 copy-start.3
  440.0 3.5 copy-start.1
  453.6 3.9 copy-start.6
  510.6 2.2 copy-start.7
  519.4 1.8 copy-start.3
  526.7 3.5 copy-start.1
  540.4 3.9 copy-start.6
  575.6 5.4 copy-start
  582.8 168.4 %reduce-scatter.5.cloned.1.call-start = ((), (), s32[]{:S(2)}) async-start(), calls=%async_computation.7 | async-start | bytes 4014080 | tf_op jit(solution)/shard_map/reduce_scatter | solution.py:197
  593.5 1.8 copy-start.34
  593.5 268.3 %reduce-scatter.3.cloned.1.call-start = ((), (), s32[]{:S(2)}) async-start(), calls=%async_computation.5 | async-start | bytes 4014080 | tf_op jit(solution)/shard_map/reduce_scatter | solution.py:171
  603.3 148.0 %copy-start.10 = (bf16[392,1024]{1,0:T(8,128)(2,1)S(1)}, bf16[392,1024]{1,0:T(8,128)(2,1)}, u32[]{:S(2)}) copy-start(bf16[392,1024]{1,0:T(8,128)(2,1)} %param.15) | copy-start | bytes 2408452
  603.3 148.0 %copy-start.23 = (f32[1024]{0:T(1024)S(1)}, f32[1024]{0:T(1024)}, u32[]{:S(2)}) copy-start(f32[1024]{0:T(1024)} %copy-done.22) | copy-start | bytes 12292
  603.3 148.0 %copy-start.25 = (f32[392]{0:T(512)S(1)}, f32[392]{0:T(512)}, u32[]{:S(2)}) copy-start(f32[392]{0:T(512)} %copy-done.24) | copy-start | bytes 4708
  603.3 149.6 %copy-start.30 = (f32[392]{0:T(512)S(1)}, f32[392]{0:T(512)}, u32[]{:S(2)}) copy-start(f32[392]{0:T(512)} %copy-done.29) | copy-start | bytes 4708
  603.3 149.6 %copy-start.28 = (f32[392]{0:T(512)S(1)}, f32[392]{0:T(512)}, u32[]{:S(2)}) copy-start(f32[392]{0:T(512)} %copy-done.27) | copy-start | bytes 4708
  691.2 62.7 %copy-start.31 = (f32[128]{0:T(128)S(1)}, f32[128]{0:T(128)}, u32[]{:S(2)}) copy-start(f32[128]{0:T(128)} %get-tuple-element.203) | copy-start | bytes 1540
  692.5 108.2 %copy-start.16 = (f32[128,1280]{1,0:T(8,128)S(1)}, f32[128,1280]{1,0:T(8,128)}, u32[]{:S(2)}) copy-start(f32[128,1280]{1,0:T(8,128)} %param.20) | copy-start | bytes 1966084
  751.3 1.7 copy-start.14
  800.7 3.8 copy-start.13
  800.7 3.8 copy-start.20
  800.7 3.8 copy-start.21
  804.5 46.9 %copy-start.26 = (f32[1152]{0:T(1024)S(1)}, f32[1152]{0:T(1024)}, u32[]{:S(2)}) copy-start(f32[1152]{0:T(1024)} %param.23) | copy-start | bytes 13828
  804.5 46.9 %copy-start.32 = (f32[1152]{0:T(1024)S(1)}, f32[1152]{0:T(1024)}, u32[]{:S(2)}) copy-start(f32[1152]{0:T(1024)} %param.25) | copy-start | bytes 13828
  804.5 46.9 %copy-start.33 = (f32[1152]{0:T(1024)S(1)}, f32[1152]{0:T(1024)}, u32[]{:S(2)}) copy-start(f32[1152]{0:T(1024)} %param.24) | copy-start | bytes 13828
  857.4 2.7 copy-start.17
  857.4 2.7 copy-start.18
  860.2 1.6 copy-start.19
  (21 other events, 22.8 us)
Sparse Core Ops, SparseCore 0:
  14.0 67.2 all-gather.4
  83.8 33.7 all-gather.6
  120.1 30.4 all-gather.8
  152.0 64.5 all-gather.10
  582.9 104.5 all-reduce.8
  689.8 61.3 reduce-scatter.4
  753.6 62.3 reduce-scatter.2
where the time goes:
time: 888 us; the launch traced here: 873 us
  waiting for transfers between devices  242 us (27%)
  local copies, waits for them, and re-layouts  193 us (22%)
  matrix products  183 us (21%)
  other arithmetic  135 us (15%)
  blocking collectives  84.2 us (9%)
  between operations  25.5 us (3%)
  loops' own time  9.52 us (1%)
    psum x2, blocking collectives, on_device(): lax.psum((jnp.sum(in_grad * in_grad), jnp.sum(out_grad * out_grad), jnp.s...  84.2 us
    psum x1, waiting for transfers between devices, on_device(): lax.psum(in_acc.astype(jnp.bfloat16), 'dp').astype(jnp.float32)  82.8 us
    reshape x40, local copies, waits for them, and re-layouts, per_image(): values.astype(jnp.bfloat16)  71.7 us
    all_gather x1, waiting for transfers between devices, on_device(): normed_all = lax.all_gather(normed, 'mp', axis=0, tiled=True)  63.3 us
    reduce_scatter x1, waiting for transfers between devices, on_device(): lax.psum_scatter(lax.dot_general(block, in_weight, (((1,), (1,)), ((), ()...  58.8 us
    all_gather x1, waiting for transfers between devices, on_device(): lax.all_gather(in_master.astype(jnp.bfloat16), 'dp', axis=0, tiled=True)  36.2 us
    dot_general x4, matrix products, back_block(): lax.dot_general(normed_block, joined_low, by_rows, preferred_element_type...  31.6 us
    reduce_sum x14, other arithmetic, layer_norm(): return centered * lax.rsqrt(variance + norm_eps) * gain  31.2 us
  transfers between devices with their start and end apart: 7, of which 4 were waited for; matrix products, arithmetic and copies ran while one was open for 17% of the time, Pallas kernels for 0%

commit v1 on v0

v1 whole, which is shorter than its diff:
```python
import functools
import math

import jax
import jax.numpy as jnp
from jax import lax
from jax.experimental import pallas as pl
from jax.experimental.pallas import tpu as pltpu
from jax.sharding import PartitionSpec as P

D = 1024
DH = 64
PATCHES = 196
STEP = 10
UNITS = 256
HEAD_IN = 3 * DH + UNITS
HEAD_OUT = DH + UNITS
PAIR_IN = 2 * HEAD_IN
PAIR_OUT = 2 * HEAD_OUT
PAIR = PAIR_IN + PAIR_OUT
ROWS = 208

norm_eps = 1e-06
lamb_eps = 1e-06
beta_first = 0.5
beta_second = 0.5
rate_step = 0.5
decay_matrix = 0.01

f32 = jnp.float32
bf16 = jnp.bfloat16
NN = (((1,), (0,)), ((), ()))
NT = (((1,), (1,)), ((), ()))
TN = (((0,), (0,)), ((), ()))
ANY = pl.BlockSpec(memory_space=pl.ANY)
VMEM = pl.BlockSpec(memory_space=pltpu.VMEM)
SMEM = pl.BlockSpec(memory_space=pltpu.SMEM)


def shape(rows, columns, kind):
    return jax.ShapeDtypeStruct((rows, columns), kind)


def params(mib):
    return pltpu.CompilerParams(vmem_limit_bytes=mib * 2**20)


def dot(a, b, dims=NN):
    return lax.dot_general(a, b, dims, preferred_element_type=f32)


def pair_in(values, pair):
    base = [(2 * pair + h) * HEAD_IN for h in range(2)]
    cuts = []
    for start, width in ((0, DH), (DH, DH), (2 * DH, DH), (3 * DH, UNITS)):
        cuts += [values[:, b + start : b + start + width] for b in base]
    return cuts


def pair_out(values, pair):
    base = [(2 * pair + h) * HEAD_OUT for h in range(2)]
    cuts = []
    for start, width in ((0, DH), (DH, UNITS)):
        cuts += [values[:, b + start : b + start + width] for b in base]
    return cuts


def heads_in(values):
    cuts = []
    for h in range(2):
        for start, width in ((0, DH), (2 * DH, DH), (4 * DH, DH), (6 * DH, UNITS)):
            at = start + h * width
            cuts.append(values[:, at : at + width])
    return cuts


def heads_out(values):
    cuts = []
    for h in range(2):
        for start, width in ((0, DH), (2 * DH, UNITS)):
            at = PAIR_IN + start + h * width
            cuts.append(values[:, at : at + width])
    return cuts


def pack_kernel(pairs, in_ref, out_ref, *outs):
    for p in range(pairs):
        packed = jnp.concatenate(pair_in(in_ref, p) + pair_out(out_ref, p), axis=1)
        outs[p][...] = packed.astype(bf16)


def pack(in_master, out_master, pairs):
    rows = in_master.shape[0]
    return pl.pallas_call(
        functools.partial(pack_kernel, pairs),
        out_shape=[shape(rows, PAIR, bf16)] * pairs,
        in_specs=[VMEM, VMEM],
        out_specs=[VMEM] * pairs,
        compiler_params=params(20),
    )(in_master, out_master)


def store_padded(out, at, values):
    images = values.shape[0] // PATCHES
    fill = jnp.zeros((ROWS - PATCHES, values.shape[1]), values.dtype)
    for i in range(images):
        block = jnp.concatenate([values[i * PATCHES : (i + 1) * PATCHES], fill], axis=0)
        out[at + i * ROWS : at + (i + 1) * ROWS, :] = block.astype(out.dtype)


def norm_kernel(own, other, gain, out):
    for k, ref in enumerate((own, other)):
        rows = ref[...].astype(f32)
        centered = rows - jnp.mean(rows, axis=1, keepdims=True)
        variance = jnp.mean(centered * centered, axis=1, keepdims=True)
        normed = centered * lax.rsqrt(variance + norm_eps) * gain[...]
        store_padded(out, k * out.shape[0] // 2, normed)


def pad_kernel(own, other, out):
    for k, ref in enumerate((own, other)):
        store_padded(out, k * out.shape[0] // 2, ref[...].astype(f32))


def padded_rows(tokens):
    return tokens.shape[0] // PATCHES * ROWS


def norm_rows(own, other, ln_gain):
    return pl.pallas_call(
        norm_kernel,
        out_shape=shape(2 * padded_rows(own), D, bf16),
        in_specs=[VMEM] * 3,
        out_specs=VMEM,
        compiler_params=params(24),
    )(own, other, ln_gain.reshape(1, D))


def pad_rows(own, other):
    return pl.pallas_call(
        pad_kernel,
        out_shape=shape(2 * padded_rows(own), D, bf16),
        in_specs=[VMEM] * 2,
        out_specs=VMEM,
        compiler_params=params(24),
    )(own, other)


def group_mean(values, averaging):
    high = values.astype(bf16)
    rest = (values - high.astype(f32)).astype(bf16)
    return dot(high, averaging) + dot(rest, averaging)


def tiles(width):
    return [(n, min(256, width - n)) for n in range(0, width, 256)]


def attention_part(images, gain, u, dz, z, du):
    row_group = lax.broadcasted_iota(jnp.int32, (4 * DH, 4 * DH), 0) // DH
    column_group = lax.broadcasted_iota(jnp.int32, (4 * DH, 4 * DH), 1) // DH
    averaging = jnp.where(row_group == column_group, 1.0 / DH, 0.0).astype(bf16)
    lane = lax.broadcasted_iota(jnp.int32, (1, 2 * DH), 1)
    of_head = (lane < DH, lane >= DH)
    none = jnp.zeros((), bf16)
    key_row = lax.broadcasted_iota(jnp.int32, (ROWS, ROWS), 0)
    scale = 1.0 / math.sqrt(DH)

    def image(i, gain_sum):
        at = pl.ds(pl.multiple_of(i * ROWS, ROWS), ROWS)
        x = u[at, 0 : 4 * DH]
        centered = x - group_mean(x, averaging)
        rstd = lax.rsqrt(group_mean(centered * centered, averaging) + norm_eps)
        normed = centered * rstd
        both = (normed * gain).astype(bf16)
        query, keys = both[:, : 2 * DH], both[:, 2 * DH :]
        values = u[at, 4 * DH : 6 * DH].astype(bf16)
        grad = dz[at, 0 : 2 * DH].astype(bf16)
        sums = None
        for head in range(2):
            keys_h = jnp.where(of_head[head], keys, none)
            values_h = jnp.where(of_head[head], values, none)
            query_h = jnp.where(of_head[head], query, none)
            grad_h = jnp.where(of_head[head], grad, none)
            scores = jnp.where(key_row < PATCHES, dot(keys_h, query, NT), -1e30)
            top = jnp.max(scores, axis=0, keepdims=True)
            powers = jnp.exp((scores - top) * scale)
            probs = powers * (1.0 / jnp.sum(powers, axis=0, keepdims=True))
            probs_low = probs.astype(bf16)
            weighted = probs * dot(values_h, grad, NT)
            total = jnp.sum(weighted, axis=0, keepdims=True)
            score_grad = (weighted - probs * total).astype(bf16)
            terms = (
                dot(values_h, probs_low, TN),
                dot(keys_h, score_grad, TN),
                dot(score_grad, query_h),
                dot(probs_low, grad_h),
            )
            sums = terms if sums is None else [a + b for a, b in zip(sums, terms)]
        z[at, 0 : 2 * DH] = sums[0].T.astype(bf16)
        normed_grad = jnp.concatenate([sums[1].T, sums[2]], axis=1) * scale
        by_gain = normed_grad * normed
        dx = normed_grad * gain
        mean_dx = group_mean(dx, averaging)
        mean_dxn = group_mean(by_gain * gain, averaging)
        du[at, 0 : 4 * DH] = (rstd * (dx - mean_dx - normed * mean_dxn)).astype(bf16)
        du[at, 4 * DH : 6 * DH] = sums[3].astype(bf16)
        return gain_sum + jnp.sum(by_gain, axis=0, keepdims=True)

    return lax.fori_loop(0, images, image, jnp.zeros((1, 4 * DH), f32))


def hidden_part(images, u, dz, z, du):
    root = math.sqrt(2 / math.pi)

    def image(i, nothing):
        at = pl.ds(pl.multiple_of(i * ROWS, ROWS), ROWS)
        x = u[at, 6 * DH : PAIR_IN]
        square = x * x
        bent = jnp.tanh(root * (x + 0.044715 * (square * x)))
        part = 0.5 + 0.5 * bent
        z[at, 2 * DH : PAIR_OUT] = (x * part).astype(bf16)
        slope = part + 0.5 * x * (1.0 - bent * bent) * (root + 3 * 0.044715 * root * square)
        du[at, 6 * DH : PAIR_IN] = (slope * dz[at, 2 * DH : PAIR_OUT]).astype(bf16)
        return nothing

    lax.fori_loop(0, images, image, 0)


def pair_kernel(plan, *refs):
    images, piece_rows, first, last, split = plan
    refs = list(refs)
    me_ref, gain_ref, h_hbm, c_hbm = refs[:4]
    del refs[:4]
    pieces = refs[: len(piece_rows)]
    del refs[: len(piece_rows)]
    if not first:
        y_hbm, dh_hbm = refs[:2]
        del refs[:2]
    if split:
        kept, sent = refs[:2]
        del refs[:2]
    else:
        whole = refs.pop(0)
    y_out, dh_out = refs[:2]
    del refs[:2]
    if last:
        y_far, dh_far = refs[:2]
        del refs[:2]
    gain_out = refs.pop(0)
    h, c, w, u, dz, z, du, g, y, dh = refs[:10]
    del refs[:10]
    if last:
        y_low, dh_low = refs[:2]
        del refs[:2]
    sems = refs.pop(0)
    used = [0]
    half = h.shape[0] // 2

    def copy(src, dst):
        made = pltpu.make_async_copy(src, dst, sems.at[used[0]])
        used[0] += 1
        made.start()
        return made

    me = me_ref[0]
    h_copy = copy(h_hbm, h)
    piece_copies = []
    for ref, (offset, start, count, unit) in zip(pieces, piece_rows):
        if offset is None:
            at = pl.ds(start, count)
        else:
            at = pl.ds(pl.multiple_of((me ^ offset) * unit + start, 16), count)
        piece_copies.append(copy(ref, w.at[at]))
    c_copy = copy(c_hbm, c)
    if not first:
        y_copy = copy(y_hbm, y)
        dh_copy = copy(dh_hbm, dh)
    h_copy.wait()
    for made in piece_copies:
        made.wait()
    for n, k in tiles(PAIR_IN):
        u[:, n : n + k] = dot(h[...], w[:, n : n + k])
    c_copy.wait()
    for n, k in tiles(PAIR_OUT):
        dz[:, n : n + k] = dot(c[...], w[:, PAIR_IN + n : PAIR_IN + n + k])
    gain_sum = attention_part(images, gain_ref[0:1, :], u, dz, z, du)
    gain_out[...] = jnp.broadcast_to(gain_sum, gain_out.shape)
    hidden_part(images, u, dz, z, du)
    leaving = []
    if not first:
        dh_copy.wait()
    for n in range(0, D, 256):
        part = dot(du[...], w[n : n + 256, 0:PAIR_IN], NT)
        if not first:
            part = part + dh[:, n : n + 256]
        if last:
            dh_low[:, n : n + 256] = part.astype(bf16)
        else:
            dh[:, n : n + 256] = part
    if last:
        leaving.append(copy(dh_low.at[pl.ds(half, half)], dh_far))
        leaving.append(copy(dh_low.at[pl.ds(0, half)], dh_out))
    else:
        leaving.append(copy(dh, dh_out))
    if not first:
        y_copy.wait()
    for n in range(0, D, 256):
        part = dot(z[...], w[n : n + 256, PAIR_IN:PAIR], NT)
        if not first:
            part = part + y[:, n : n + 256]
        if last:
            y_low[:, n : n + 256] = part.astype(bf16)
        else:
            y[:, n : n + 256] = part
    if last:
        leaving.append(copy(y_low.at[pl.ds(half, half)], y_far))
        leaving.append(copy(y_low.at[pl.ds(0, half)], y_out))
    else:
        leaving.append(copy(y, y_out))

    def send_gradient(column, width):
        columns = pl.ds(column, width)
        if not split:
            leaving.append(copy(g.at[:, columns], whole.at[:, columns]))
            return
        unit = g.shape[0] // 8
        for k in range(4):
            to = pl.ds(k * unit, unit)
            for out, bit in ((sent, 1), (kept, 0)):
                at = pl.ds(pl.multiple_of((me ^ (2 * k + bit)) * unit, unit), unit)
                leaving.append(copy(g.at[at, columns], out.at[to, columns]))

    for n, k in tiles(PAIR_IN):
        g[:, n : n + k] = dot(h[...], du[:, n : n + k], TN).astype(bf16)
    send_gradient(0, PAIR_IN)
    for n, k in tiles(PAIR_OUT):
        g[:, PAIR_IN + n : PAIR_IN + n + k] = dot(c[...], z[:, n : n + k], TN).astype(bf16)
    send_gradient(PAIR_IN, PAIR_OUT)
    for made in leaving:
        made.wait()


def pair_step(me, gain, h, c, pieces, sums, last, split):
    rows = h.shape[0]
    first = sums is None
    arrays = [a for a, _ in pieces]
    plan = (rows // ROWS, [r for _, r in pieces], first, last, split)
    half = rows // 2
    if split:
        outs = [shape(D // 2, PAIR, bf16)] * 2
    else:
        outs = [shape(D, PAIR, bf16)]
    if last:
        outs += [shape(half, D, bf16)] * 4
    else:
        outs += [shape(rows, D, f32)] * 2
    outs.append(shape(8, 4 * DH, f32))
    scratch = [
        pltpu.VMEM((rows, D), bf16),
        pltpu.VMEM((rows, D), bf16),
        pltpu.VMEM((D, PAIR), bf16),
        pltpu.VMEM((rows, PAIR_IN), f32),
        pltpu.VMEM((rows, PAIR_OUT), f32),
        pltpu.VMEM((rows, PAIR_OUT), bf16),
        pltpu.VMEM((rows, PAIR_IN), bf16),
        pltpu.VMEM((D, PAIR), bf16),
        pltpu.VMEM((rows, D), f32),
        pltpu.VMEM((rows, D), f32),
    ]
    if last:
        scratch += [pltpu.VMEM((rows, D), bf16)] * 2
    scratch.append(pltpu.SemaphoreType.DMA((len(pieces) + 26,)))
    flops = 2 * rows * D * 3 * PAIR
    return pl.pallas_call(
        functools.partial(pair_kernel, plan),
        out_shape=outs,
        in_specs=[SMEM, VMEM] + [ANY] * (2 + len(pieces) + (0 if first else 2)),
        out_specs=[ANY] * (len(outs) - 1) + [VMEM],
        scratch_shapes=scratch,
        compiler_params=params(48),
        cost_estimate=pl.CostEstimate(flops=flops, bytes_accessed=20 * 2**20, transcendentals=0),
    )(me, gain, h, c, *arrays, *(() if first else sums))


def over_dp(values, bit):
    return lax.ppermute(values, "dp", [(i, i ^ bit) for i in range(lax.axis_size("dp"))])


def over_mp(values, bit):
    return lax.ppermute(values, "mp", [(i, i ^ bit) for i in range(lax.axis_size("mp"))])


def gather_pieces(own):
    count = own.shape[0]
    if lax.axis_size("dp") != 8:
        full = lax.all_gather(own, "dp", axis=0, tiled=True)
        return [(full, (None, 0, full.shape[0], 1))]
    half = count // 2
    by_x = over_dp(own, 2)
    by_y = over_dp(own, 4)
    far_top = over_dp(by_x[:half], 4)
    far_low = over_dp(by_y[half:], 2)
    mine = [
        (own, (0, 0, count, count)),
        (by_x, (2, 0, count, count)),
        (by_y, (4, 0, count, count)),
        (far_top, (6, 0, half, count)),
        (far_low, (6, half, half, count)),
    ]
    theirs = [
        (over_dp(values, 1), (at[0] ^ 1, at[1], at[2], at[3])) for values, at in mine
    ]
    return mine + theirs


def add(*values):
    total = values[0].astype(f32)
    for value in values[1:]:
        total = total + value.astype(f32)
    return total


def scatter_sum(kept, sent):
    unit = kept.shape[0] // 4
    half = unit // 2
    got = over_dp(sent, 1)
    far = add(kept[3 * unit :], got[3 * unit :]).astype(bf16)
    top = over_dp(far[:half], 2)
    low = over_dp(far[half:], 4)
    nothing = jnp.zeros_like(top)
    for_x = add(kept[unit : 2 * unit], got[unit : 2 * unit], jnp.concatenate([nothing, low]))
    for_y = add(kept[2 * unit : 3 * unit], got[2 * unit : 3 * unit], jnp.concatenate([top, nothing]))
    by_x = over_dp(for_x.astype(bf16), 2)
    by_y = over_dp(for_y.astype(bf16), 4)
    return add(kept[:unit], got[:unit], by_x, by_y)


def sum_all(values):
    count = lax.axis_size("dp") * lax.axis_size("mp")
    copies = jnp.broadcast_to(values[None], (count,) + values.shape)
    return jnp.sum(lax.all_to_all(copies, ("dp", "mp"), 0, 0), axis=0)


def unpadded(values):
    images = values.shape[0] // ROWS
    return jnp.concatenate([values[i * ROWS : i * ROWS + PATCHES] for i in range(images)], axis=0)


def output_kernel(tokens, own, other, out):
    branch = own[...].astype(f32) + other[...].astype(f32)
    out[...] = (tokens[...].astype(f32) + unpadded(branch)).astype(bf16)


def block_output(tokens, own, other):
    return pl.pallas_call(
        output_kernel,
        out_shape=shape(*tokens.shape, bf16),
        in_specs=[VMEM] * 3,
        out_specs=VMEM,
        compiler_params=params(24),
    )(tokens, own, other)


def input_kernel(tokens, cotangent, gain, own, other, out, gain_grad):
    grad = unpadded(own[...].astype(f32) + other[...].astype(f32))
    rows = tokens[...].astype(f32)
    centered = rows - jnp.mean(rows, axis=1, keepdims=True)
    variance = jnp.mean(centered * centered, axis=1, keepdims=True)
    rstd = lax.rsqrt(variance + norm_eps)
    normed = centered * rstd
    by_gain = grad * normed
    gain_grad[...] = jnp.broadcast_to(jnp.sum(by_gain, axis=0, keepdims=True), gain_grad.shape)
    dx = grad * gain[...]
    mean_dx = jnp.mean(dx, axis=1, keepdims=True)
    mean_dxn = jnp.mean(by_gain * gain[...], axis=1, keepdims=True)
    rows_grad = rstd * (dx - mean_dx - normed * mean_dxn)
    out[...] = (cotangent[...].astype(f32) + rows_grad).astype(bf16)


def input_gradient(tokens, cotangent, ln_gain, own, other):
    return pl.pallas_call(
        input_kernel,
        out_shape=[shape(*tokens.shape, bf16), shape(8, D, f32)],
        in_specs=[VMEM] * 5,
        out_specs=[VMEM] * 2,
        compiler_params=params(32),
    )(tokens, cotangent, ln_gain.reshape(1, D), own, other)


def moments(grad, first, second, weight, decay):
    first_new = beta_first * first + (1.0 - beta_first) * grad
    second_new = beta_second * second + (1.0 - beta_second) * grad * grad
    first_hat = first_new / (1.0 - beta_first**STEP)
    second_hat = second_new / (1.0 - beta_second**STEP)
    update = first_hat / (jnp.sqrt(second_hat) + lamb_eps) + decay * weight
    return (first_new, second_new, update)


def moment_kernel(pairs, factor_ref, *refs):
    grads, refs = refs[:pairs], refs[pairs:]
    factor = factor_ref[0]
    sums = []
    for k, cut in enumerate((heads_in, heads_out)):
        master, first, second = refs[3 * k : 3 * k + 3]
        first_out, second_out, update_out = refs[6 + 3 * k : 9 + 3 * k]
        grad = jnp.concatenate([part for g in grads for part in cut(g[...])], axis=1)
        first_new, second_new, update = moments(
            grad * factor, first[...], second[...], master[...], decay_matrix
        )
        first_out[...] = first_new
        second_out[...] = second_new
        update_out[...] = update
        sums.append(jnp.sum(update * update, axis=0, keepdims=True))
    in_sum, out_sum = refs[12:]

    @pl.when(pl.program_id(0) == 0)
    def _():
        in_sum[...] = jnp.zeros_like(in_sum)
        out_sum[...] = jnp.zeros_like(out_sum)

    in_sum[...] += jnp.broadcast_to(sums[0], in_sum.shape)
    out_sum[...] += jnp.broadcast_to(sums[1], out_sum.shape)


def moment_step(factor, grads, in_state, out_state):
    rows, in_width = in_state[0].shape
    out_width = out_state[0].shape[1]
    step = 32

    def block(width):
        return pl.BlockSpec((step, width), lambda i: (i, 0))

    def total(width):
        return pl.BlockSpec((8, width), lambda i: (0, 0))

    pairs = len(grads)
    return pl.pallas_call(
        functools.partial(moment_kernel, pairs),
        grid=(rows // step,),
        out_shape=[shape(rows, in_width, f32)] * 3
        + [shape(rows, out_width, f32)] * 3
        + [shape(8, in_width, f32), shape(8, out_width, f32)],
        in_specs=[SMEM] + [block(PAIR)] * pairs + [block(in_width)] * 3 + [block(out_width)] * 3,
        out_specs=[block(in_width)] * 3
        + [block(out_width)] * 3
        + [total(in_width), total(out_width)],
        compiler_params=params(32),
    )(factor, *grads, *in_state, *out_state)


def trust_kernel(rates, in_master, in_update, out_master, out_update, in_new, in_low, out_new, out_low):
    in_value = in_master[...] - rates[0] * in_update[...]
    in_new[...] = in_value
    in_low[...] = in_value.astype(bf16)
    out_value = out_master[...] - rates[1] * out_update[...]
    out_new[...] = out_value
    out_low[...] = out_value.astype(bf16)


def trust_steps(rates, in_master, in_update, out_master, out_update):
    rows, in_width = in_master.shape
    out_width = out_master.shape[1]
    step = 32

    def block(width):
        return pl.BlockSpec((step, width), lambda i: (i, 0))

    return pl.pallas_call(
        trust_kernel,
        grid=(rows // step,),
        out_shape=[
            shape(rows, in_width, f32),
            shape(rows, in_width, bf16),
            shape(rows, out_width, f32),
            shape(rows, out_width, bf16),
        ],
        in_specs=[SMEM] + [block(in_width)] * 2 + [block(out_width)] * 2,
        out_specs=[block(in_width)] * 2 + [block(out_width)] * 2,
        compiler_params=params(32),
    )(rates, in_master, in_update, out_master, out_update)


def local_trust(weight, update):
    weight_norm = jnp.sqrt(jnp.sum(weight * weight))
    update_norm = jnp.sqrt(jnp.sum(update * update))
    return (weight_norm, update_norm, weight - rate_step * (weight_norm / update_norm) * update)


def on_device(
    tokens,
    cotangent,
    in_master,
    in_first,
    in_second,
    out_master,
    out_first,
    out_second,
    gains,
    gain_first,
    gain_second,
):
    ln_gain = gains[:D]
    q_gain = gains[D : D + DH]
    k_gain = gains[D + DH :]
    pairs = in_master.shape[1] // PAIR_IN
    split = lax.axis_size("dp") == 8
    me = lax.axis_index("dp").astype(jnp.int32).reshape(1)
    pair_gain = jnp.broadcast_to(
        jnp.concatenate([q_gain, q_gain, k_gain, k_gain]).reshape(1, 4 * DH), (8, 4 * DH)
    )

    tokens_other = over_mp(tokens, 1)
    packed = pack(in_master, out_master, pairs)
    cotangent_other = over_mp(cotangent, 1)
    h = norm_rows(tokens, tokens_other, ln_gain)
    c = pad_rows(cotangent, cotangent_other)

    others = [(delta, p) for delta in range(2, lax.axis_size("mp"), 2) for p in range(pairs)]
    order = [(0, 0)] + others + [(0, p) for p in range(1, pairs)]
    sums = None
    gain_sums = []
    grads = [[] for _ in range(pairs)]
    for k, (delta, p) in enumerate(order):
        own = packed[p] if delta == 0 else over_mp(packed[p], delta)
        pieces = gather_pieces(own)
        last = k == len(order) - 1
        outs = pair_step(me, pair_gain, h, c, pieces, sums, last, split)
        gain_sums.append(outs[-1][0])
        if split:
            grad = scatter_sum(outs[0], outs[1])
            rest = outs[2:-1]
        else:
            grad = lax.psum_scatter(outs[0], "dp", scatter_dimension=0, tiled=True).astype(f32)
            rest = outs[1:-1]
        if delta:
            grad = over_mp(grad.astype(bf16), delta).astype(f32)
        grads[p].append(grad)
        if last:
            y_own, dh_own, y_far, dh_far = rest
        else:
            sums = rest

    dh_other = over_mp(dh_far, 1)
    y_other = over_mp(y_far, 1)
    block_out = block_output(tokens, y_own, y_other)
    input_grad, ln_grad = input_gradient(tokens, cotangent, ln_gain, dh_own, dh_other)

    total_grads = [add(*parts) for parts in grads]
    norm_grad = sum(gain_sums)
    q_grad = norm_grad[:DH] + norm_grad[DH : 2 * DH]
    k_grad = norm_grad[2 * DH : 3 * DH] + norm_grad[3 * DH :]
    matrix_square = sum(jnp.sum(g * g) for g in total_grads)
    scalars = jnp.stack(
        [matrix_square, jnp.sum(in_master * in_master), jnp.sum(out_master * out_master)]
    )
    message = jnp.concatenate([ln_grad[0], q_grad, k_grad, scalars])
    message = jnp.pad(message, (0, 2048 - message.shape[0])).reshape(16, 128)
    message = sum_all(message).reshape(2048)
    gain_grad = message[: D + 2 * DH]
    squares = message[D + 2 * DH : D + 2 * DH + 3]
    grad_norm = jnp.sqrt(squares[0] + jnp.sum(gain_grad * gain_grad))
    factor = 1.0 / jnp.maximum(grad_norm, 1.0)
    (
        in_first_new,
        in_second_new,
        in_update,
        out_first_new,
        out_second_new,
        out_update,
        in_sum,
        out_sum,
    ) = moment_step(
        factor.reshape(1),
        total_grads,
        (in_master, in_first, in_second),
        (out_master, out_first, out_second),
    )
    gain_first_new, gain_second_new, gain_update = moments(
        gain_grad * factor, gain_first, gain_second, gains, 0.0
    )
    update_squares = jnp.stack([jnp.sum(in_sum[0]), jnp.sum(out_sum[0])])
    update_squares = sum_all(jnp.broadcast_to(update_squares[:, None], (2, 128)))[:, 0]
    in_wnorm = jnp.sqrt(squares[1])
    in_unorm = jnp.sqrt(update_squares[0])
    out_wnorm = jnp.sqrt(squares[2])
    out_unorm = jnp.sqrt(update_squares[1])
    rates = jnp.stack([rate_step * (in_wnorm / in_unorm), rate_step * (out_wnorm / out_unorm)])
    in_master_new, in_copy, out_master_new, out_copy = trust_steps(
        rates, in_master, in_update, out_master, out_update
    )
    ln_wnorm, ln_unorm, ln_new = local_trust(gains[:D], gain_update[:D])
    q_wnorm, q_unorm, q_new = local_trust(gains[D : D + DH], gain_update[D : D + DH])
    k_wnorm, k_unorm, k_new = local_trust(gains[D + DH :], gain_update[D + DH :])
    gains_new = jnp.concatenate([ln_new, q_new, k_new])
    norm_table = jnp.stack(
        [
            jnp.stack([in_wnorm, in_unorm]),
            jnp.stack([out_wnorm, out_unorm]),
            jnp.stack([ln_wnorm, ln_unorm]),
            jnp.stack([q_wnorm, q_unorm]),
            jnp.stack([k_wnorm, k_unorm]),
        ]
    )
    return (
        block_out,
        input_grad,
        in_first_new,
        in_second_new,
        in_master_new,
        in_copy,
        out_first_new,
        out_second_new,
        out_master_new,
        out_copy,
        gain_first_new,
        gain_second_new,
        gains_new,
        grad_norm,
        norm_table,
    )


def solution(mesh):
    rows = P(("dp", "mp"), None)
    matrix = P("dp", "mp")
    in_specs = (rows, rows) + (matrix,) * 6 + (P(),) * 3
    out_specs = (rows, rows) + (matrix,) * 8 + (P(),) * 5
    return jax.shard_map(
        on_device, mesh=mesh, in_specs=in_specs, out_specs=out_specs, check_vma=False
    )
```

time: 888 us -> 353 us (0.40); the launches traced: 873 us -> 348 us
  matrix products: 183 us -> 0 us
  local copies, waits for them, and re-layouts: 193 us -> 30.9 us
  other arithmetic: 135 us -> 16.4 us
  waiting for transfers between devices: 242 us -> 129 us
  Pallas kernels: 0 us -> 105 us
  blocking collectives: 84.2 us -> 0 us
  starting transfers between devices: 0.28 us -> 55.3 us
  between operations: 25.5 us -> 12.4 us
  loops' own time: 9.52 us -> 0 us
    dot_general x42 -> x0, matrix products: 159 us -> none  [the longest x4 31.6 us: back_block(): lax.dot_general(normed_block, joined_low, by_rows, preferred_element_type...]
    reshape x72 -> x0, local copies, waits for them, and re-layouts: 134 us -> none  [the longest x40 71.7 us: per_image(): values.astype(jnp.bfloat16)]
    ppermute x0 -> x64, waiting for transfers between devices: none -> 122 us  [the longest x56 65.5 us: over_dp(): lax.ppermute(values, 'dp', [(i, i ^ bit) for i in range(lax.axis_size('dp...]
    pallas_call x0 -> x11, Pallas kernels: none -> 105 us  [the longest x4 90.3 us: pair_step(): pl.pallas_call(functools.partial(pair_kernel, plan), out_shape=outs, in_s...]
    all_gather x4 -> x0, waiting for transfers between devices: 99.5 us -> none  [the longest x1 63.3 us: on_device(): normed_all = lax.all_gather(normed, 'mp', axis=0, tiled=True)]
    psum x2 -> x0, blocking collectives: 84.2 us -> none  [on_device(): lax.psum((jnp.sum(in_grad * in_grad), jnp.sum(out_grad * out_grad), jnp.s...]
    psum x1 -> x0, waiting for transfers between devices: 82.8 us -> none  [on_device(): lax.psum(in_acc.astype(jnp.bfloat16), 'dp').astype(jnp.float32)]
    reduce_scatter x2 -> x0, waiting for transfers between devices: 58.8 us -> none  [the longest x1 58.8 us: on_device(): lax.psum_scatter(lax.dot_general(block, in_weight, (((1,), (1,)), ((), ()...]
  transfers between devices with their start and end apart: 7 -> 66, of which waited for: 4 -> 23; matrix products, arithmetic and copies ran while one was open for 17% -> 5% of each run, Pallas kernels for 0% -> 28%
where the time goes in v1:
time: 353 us; the launch traced here: 348 us
  waiting for transfers between devices  129 us (37%)
  Pallas kernels  105 us (30%)
  starting transfers between devices  55.3 us (16%)
  local copies, waits for them, and re-layouts  30.9 us (9%)
  other arithmetic  16.4 us (5%)
  between operations  12.4 us (4%)
    pallas_call x4, Pallas kernels, pair_step(): pl.pallas_call(functools.partial(pair_kernel, plan), out_shape=outs, in_s...  90.3 us
    ppermute x56, waiting for transfers between devices, over_dp(): lax.ppermute(values, 'dp', [(i, i ^ bit) for i in range(lax.axis_size('dp...  65.5 us
    ppermute x8, waiting for transfers between devices, over_mp(): lax.ppermute(values, 'mp', [(i, i ^ bit) for i in range(lax.axis_size('mp...  56.1 us
    ppermute x56, starting transfers between devices, over_dp(): lax.ppermute(values, 'dp', [(i, i ^ bit) for i in range(lax.axis_size('dp...  35.9 us
    unnamed x100, local copies, waits for them, and re-layouts  21.3 us
    ppermute x8, starting transfers between devices, over_mp(): lax.ppermute(values, 'mp', [(i, i ^ bit) for i in range(lax.axis_size('mp...  12.4 us
  transfers between devices with their start and end apart: 66, of which 23 were waited for; matrix products, arithmetic and copies ran while one was open for 5% of the time, Pallas kernels for 28%

profile of v1, /device:TPU:0, one launch (start us, length us, event | category | flops | bytes accessed | tf_op | source)
XLA Modules:
  0.0 348.0 jit_solution(5834797510908999901)
XLA Ops:
  3.2 3.0 collective-permute-start.31
  6.2 1.5 collective-permute-start.32
  7.7 2.6 collective-permute-start.21
  11.5 3.7 %collective-permute-done.31.refs_5_ = bf16[128,1536]{1,0:T(8,128)(2,1)S(1)} collective-permute-done((bf16[128,1536]{1,0:T(8,128)(2,1)S(1)}, bf16[128,1536]{1,0:T(8,128)(2,1)S(1)}, u32[]{:S(2)}, u32[]{:S(2)}) %collective-permute-start.31) | collective-permute-done | bytes 393248 | tf_op jit(solution)/shard_map/ppermute | solution.py:387
  15.3 2.8 collective-permute-start.11
  18.2 1.4 collective-permute-start.2
  20.4 17.1 %collective-permute-done.21.refs_4_ = bf16[128,1536]{1,0:T(8,128)(2,1)} collective-permute-done((bf16[128,1536]{1,0:T(8,128)(2,1)S(1)}, bf16[128,1536]{1,0:T(8,128)(2,1)}, u32[]{:S(2)}, u32[]{:S(2)}) %collective-permute-start.21) | collective-permute-done | bytes 393248 | tf_op jit(solution)/shard_map/ppermute | solution.py:391
  38.4 7.1 %collective-permute-done.11.refs_4_ = bf16[128,1536]{1,0:T(8,128)(2,1)} collective-permute-done((bf16[128,1536]{1,0:T(8,128)(2,1)S(1)}, bf16[128,1536]{1,0:T(8,128)(2,1)}, u32[]{:S(2)}, u32[]{:S(2)}) %collective-permute-start.11) | collective-permute-done | bytes 393248 | tf_op jit(solution)/shard_map/ppermute | solution.py:391
  47.8 4.2 %collective-permute-done.5.refs_8_ = bf16[64,1536]{1,0:T(8,128)(2,1)S(1)} collective-permute-done((bf16[64,1536]{1,0:T(8,128)(2,1)S(1)}, bf16[64,1536]{1,0:T(8,128)(2,1)S(1)}, u32[]{:S(2)}, u32[]{:S(2)}) %collective-permute-start.5) | collective-permute-done | bytes 196640 | tf_op jit(solution)/shard_map/ppermute | solution.py:387
  54.8 1.4 collective-permute-start.1
  57.0 1.5 collective-permute-start.22
  61.6 7.7 %collective-permute-done.22.refs_5_ = bf16[128,1536]{1,0:T(8,128)(2,1)} collective-permute-done((bf16[128,1536]{1,0:T(8,128)(2,1)}, bf16[128,1536]{1,0:T(8,128)(2,1)}, u32[]{:S(2)}, u32[]{:S(2)}) %collective-permute-start.22) | collective-permute-done | bytes 393248 | tf_op jit(solution)/shard_map/ppermute | solution.py:387
  70.6 5.2 %collective-permute-done.12.refs_5_ = bf16[128,1536]{1,0:T(8,128)(2,1)} collective-permute-done((bf16[128,1536]{1,0:T(8,128)(2,1)}, bf16[128,1536]{1,0:T(8,128)(2,1)}, u32[]{:S(2)}, u32[]{:S(2)}) %collective-permute-start.12) | collective-permute-done | bytes 393248 | tf_op jit(solution)/shard_map/ppermute | solution.py:387
  81.3 9.1 %collective-permute-done.1.other = bf16[392,1024]{1,0:T(8,128)(2,1)} collective-permute-done((bf16[392,1024]{1,0:T(8,128)(2,1)S(1)}, bf16[392,1024]{1,0:T(8,128)(2,1)}, u32[]{:S(2)}, u32[]{:S(2)}) %collective-permute-start.1) | collective-permute-done | bytes 802848 | tf_op jit(solution)/shard_map/ppermute | solution.py:391
  92.4 1.4 shard_map.227.refs_3_
  95.0 2.5 shard_map.226.refs_2_
  100.9 22.6 %shard_map.229 = (bf16[512,1536]{1,0:T(8,128)(2,1)S(1)}, bf16[512,1536]{1,0:T(8,128)(2,1)}, f32[832,1024]{1,0:T(8,128)}, f32[832,1024]{1,0:T(8,128)}, f32[8,256]{1,0:T(8,128)S(1)}) custom-call(s32[1]{0:T(128)} %bitcast.refs_0_, f32[8,256]{1,0:T(8,128)S(1)} %broadcast_in_dim.6.refs_1_, bf16[832,1024]{1,0:T(8,128)(2,1)} %copy-done.8, ...), custom_call_target="tpu_custom_call" | custom-call | flops 7851737088 | bytes 20971520 | tf_op jit(solution)/shard_map/pallas_call | solution.py:375
  124.7 22.5 %shard_map.230 = (bf16[512,1536]{1,0:T(8,128)(2,1)S(1)}, bf16[512,1536]{1,0:T(8,128)(2,1)}, f32[832,1024]{1,0:T(8,128)}, f32[832,1024]{1,0:T(8,128)}, f32[8,256]{1,0:T(8,128)S(1)}) custom-call(s32[1]{0:T(128)} %bitcast.refs_0_, f32[8,256]{1,0:T(8,128)S(1)} %broadcast_in_dim.6.refs_1_, bf16[832,1024]{1,0:T(8,128)(2,1)} %copy-done.8, ...), custom_call_target="tpu_custom_call" | custom-call | flops 7851737088 | bytes 20971520 | tf_op jit(solution)/shard_map/pallas_call | solution.py:375
  148.3 22.5 %shard_map.231 = (bf16[512,1536]{1,0:T(8,128)(2,1)S(1)}, bf16[512,1536]{1,0:T(8,128)(2,1)}, f32[832,1024]{1,0:T(8,128)}, f32[832,1024]{1,0:T(8,128)}, f32[8,256]{1,0:T(8,128)S(1)}) custom-call(s32[1]{0:T(128)} %bitcast.refs_0_, f32[8,256]{1,0:T(8,128)S(1)} %broadcast_in_dim.6.refs_1_, bf16[832,1024]{1,0:T(8,128)(2,1)} %copy-done.8, ...), custom_call_target="tpu_custom_call" | custom-call | flops 7851737088 | bytes 20971520 | tf_op jit(solution)/shard_map/pallas_call | solution.py:375
  171.3 22.8 %shard_map.232 = (bf16[512,1536]{1,0:T(8,128)(2,1)}, bf16[512,1536]{1,0:T(8,128)(2,1)}, bf16[416,1024]{1,0:T(8,128)(2,1)S(1)}, bf16[416,1024]{1,0:T(8,128)(2,1)S...) custom-call(s32[1]{0:T(128)} %bitcast.refs_0_, ...), custom_call_target="tpu_custom_call" | custom-call | flops 7851737088 | bytes 20971520 | tf_op jit(solution)/shard_map/pallas_call | solution.py:375
  195.8 1.6 collective-permute-start.43
  198.4 4.4 %collective-permute-done.43 = bf16[64,1536]{1,0:T(8,128)(2,1)S(1)} collective-permute-done((bf16[64,1536]{1,0:T(8,128)(2,1)S(1)}, bf16[64,1536]{1,0:T(8,128)(2,1)S(1)}, u32[]{:S(2)}, u32[]{:S(2)}) %collective-permute-start.43) | collective-permute-done | bytes 196640 | tf_op jit(solution)/shard_map/ppermute | solution.py:387
  204.0 1.4 add_convert_fusion.12
  206.5 1.3 collective-permute-start.54
  210.0 4.1 %collective-permute-done.54 = bf16[64,1536]{1,0:T(8,128)(2,1)S(1)} collective-permute-done((bf16[64,1536]{1,0:T(8,128)(2,1)S(1)}, bf16[64,1536]{1,0:T(8,128)(2,1)S(1)}, u32[]{:S(2)}, u32[]{:S(2)}) %collective-permute-start.54) | collective-permute-done | bytes 196640 | tf_op jit(solution)/shard_map/ppermute | solution.py:387
  215.2 6.5 %collective-permute-done.56 = bf16[64,1536]{1,0:T(8,128)(2,1)S(1)} collective-permute-done((bf16[64,1536]{1,0:T(8,128)(2,1)S(1)}, bf16[64,1536]{1,0:T(8,128)(2,1)S(1)}, u32[]{:S(2)}, u32[]{:S(2)}) %collective-permute-start.56) | collective-permute-done | bytes 196640 | tf_op jit(solution)/shard_map/ppermute | solution.py:387
  222.8 1.4 collective-permute-start.50
  224.2 1.7 collective-permute-done.62
  227.1 2.2 collective-permute-done.48
  230.7 1.3 collective-permute-start.61
  232.3 6.9 %collective-permute-done.55 = bf16[128,1536]{1,0:T(8,128)(2,1)S(1)} collective-permute-done((bf16[128,1536]{1,0:T(8,128)(2,1)S(1)}, bf16[128,1536]{1,0:T(8,128)(2,1)S(1)}, u32[]{:S(2)}, u32[]{:S(2)}) %collective-permute-start.55) | collective-permute-done | bytes 393248 | tf_op jit(solution)/shard_map/ppermute | solution.py:387
  239.2 1.3 collective-permute-start.49
  241.5 11.8 %collective-permute-done.49 = bf16[128,1536]{1,0:T(8,128)(2,1)S(1)} collective-permute-done((bf16[128,1536]{1,0:T(8,128)(2,1)S(1)}, bf16[128,1536]{1,0:T(8,128)(2,1)S(1)}, u32[]{:S(2)}, u32[]{:S(2)}) %collective-permute-start.49) | collective-permute-done | bytes 393248 | tf_op jit(solution)/shard_map/ppermute | solution.py:387
  254.2 3.5 collective-permute-start.58
  258.6 2.3 shard_map.234
  260.9 4.5 %collective-permute-done.63 = bf16[128,1536]{1,0:T(8,128)(2,1)S(1)} collective-permute-done((bf16[128,1536]{1,0:T(8,128)(2,1)S(1)}, bf16[128,1536]{1,0:T(8,128)(2,1)S(1)}, u32[]{:S(2)}, u32[]{:S(2)}) %collective-permute-start.63) | collective-permute-done | bytes 393248 | tf_op jit(solution)/shard_map/ppermute | solution.py:387
  266.2 15.4 %collective-permute-done.58 = bf16[128,1536]{1,0:T(8,128)(2,1)S(1)} collective-permute-done((bf16[128,1536]{1,0:T(8,128)(2,1)S(1)}, bf16[128,1536]{1,0:T(8,128)(2,1)S(1)}, u32[]{:S(2)}, u32[]{:S(2)}) %collective-permute-start.58) | collective-permute-done | bytes 393248 | tf_op jit(solution)/shard_map/ppermute | solution.py:391
  282.5 7.4 %collective-permute-done.52 = bf16[128,1536]{1,0:T(8,128)(2,1)S(1)} collective-permute-done((bf16[128,1536]{1,0:T(8,128)(2,1)S(1)}, bf16[128,1536]{1,0:T(8,128)(2,1)S(1)}, u32[]{:S(2)}, u32[]{:S(2)}) %collective-permute-start.52) | collective-permute-done | bytes 393248 | tf_op jit(solution)/shard_map/ppermute | solution.py:391
  289.9 2.8 multiply_reduce_fusion.2
  293.9 1.3 concatenate.43
  296.0 4.2 %all-to-all-start = ((f32[32,16,128]{2,1,0:T(8,128)}), f32[32,16,128]{2,1,0:T(8,128)S(1)}, u32[]{:S(2)}, u32[]{:S(2)}) async-start(f32[32,16,128]{2,1,0:T(8,128)} %broadcast_in_dim.15), calls=%async_computation | async-start | bytes 524288 | tf_op jit(solution)/shard_map/all_to_all | solution.py:442
  303.4 2.4 shard_map.233
  305.9 4.5 %all-to-all-done = f32[32,16,128]{2,1,0:T(8,128)S(1)} async-done(((f32[32,16,128]{2,1,0:T(8,128)}), f32[32,16,128]{2,1,0:T(8,128)S(1)}, u32[]{:S(2)}, u32[]{:S(2)}) %all-to-all-start) | async-done | bytes 262176 | tf_op jit(solution)/shard_map/all_to_all | solution.py:442
  320.7 3.1 shard_map.235
  326.8 1.4 pad_maximum_fusion.1
  328.8 2.7 all-to-all-start.1
  336.4 2.4 all-to-all-done.1
  343.6 2.4 shard_map.236
  (260 shorter events, 66.9 us)
Async XLA Ops:
  3.2 12.1 %collective-permute-start.31 = (bf16[128,1536]{1,0:T(8,128)(2,1)S(1)}, bf16[128,1536]{1,0:T(8,128)(2,1)S(1)}, u32[]{:S(2)}, u32[]{:S(2)}) collective-permute-start(bf16[128,1536]{1,0:T(8,128)(2,1)S(1)} %get-tuple-element.54.refs_4_), channel_id=1, source_target_pairs={{0,8},{4,12},{8,0},{12,4},{16,24},{20,28},{24,16},{28,20},{1,9},{5... | collective-permute-start | bytes 1179656 | tf_op jit(solution)/shard_map/ppermute | solution.py:387
  6.2 12.0 %collective-permute-start.32 = (bf16[128,1536]{1,0:T(8,128)(2,1)S(1)}, bf16[128,1536]{1,0:T(8,128)(2,1)S(1)}, u32[]{:S(2)}, u32[]{:S(2)}) collective-permute-start(bf16[128,1536]{1,0:T(8,128)(2,1)S(1)} %get-tuple-element.54.refs_4_), channel_id=1, source_target_pairs={{0,16},{4,20},{8,24},{12,28},{16,0},{20,4},{24,8},{28,12},{1,17},{... | collective-permute-start | bytes 1179656 | tf_op jit(solution)/shard_map/ppermute | solution.py:387
  7.7 29.8 %collective-permute-start.21 = (bf16[128,1536]{1,0:T(8,128)(2,1)S(1)}, bf16[128,1536]{1,0:T(8,128)(2,1)}, u32[]{:S(2)}, u32[]{:S(2)}) collective-permute-start(bf16[128,1536]{1,0:T(8,128)(2,1)S(1)} %get-tuple-element.54.refs_4_), channel_id=1, source_target_pairs={{0,2},{1,3},{2,0},{3,1},{4,6},{5,7},{6,4},{7,5},{8,10},{9,11},{10,... | collective-permute-start | bytes 1179656 | tf_op jit(solution)/shard_map/ppermute | solution.py:391
  11.0 27.0 %collective-permute-start.3 = (bf16[128,1536]{1,0:T(8,128)(2,1)S(1)}, bf16[128,1536]{1,0:T(8,128)(2,1)S(1)}, u32[]{:S(2)}, u32[]{:S(2)}) collective-permute-start(bf16[128,1536]{1,0:T(8,128)(2,1)S(1)} %get-tuple-element.53.refs_4_), channel_id=1, source_target_pairs={{0,16},{4,20},{8,24},{12,28},{16,0},{20,4},{24,8},{28,12},{1,17},{... | collective-permute-start | bytes 1179656 | tf_op jit(solution)/shard_map/ppermute | solution.py:387
  15.3 30.2 %collective-permute-start.11 = (bf16[128,1536]{1,0:T(8,128)(2,1)S(1)}, bf16[128,1536]{1,0:T(8,128)(2,1)}, u32[]{:S(2)}, u32[]{:S(2)}) collective-permute-start(bf16[128,1536]{1,0:T(8,128)(2,1)S(1)} %get-tuple-element.53.refs_4_), channel_id=1, source_target_pairs={{0,2},{1,3},{2,0},{3,1},{4,6},{5,7},{6,4},{7,5},{8,10},{9,11},{10,... | collective-permute-start | bytes 1179656 | tf_op jit(solution)/shard_map/ppermute | solution.py:391
  18.2 27.8 %collective-permute-start.2 = (bf16[128,1536]{1,0:T(8,128)(2,1)S(1)}, bf16[128,1536]{1,0:T(8,128)(2,1)S(1)}, u32[]{:S(2)}, u32[]{:S(2)}) collective-permute-start(bf16[128,1536]{1,0:T(8,128)(2,1)S(1)} %get-tuple-element.53.refs_4_), channel_id=1, source_target_pairs={{0,8},{4,12},{8,0},{12,4},{16,24},{20,28},{24,16},{28,20},{1,9},{5... | collective-permute-start | bytes 1179656 | tf_op jit(solution)/shard_map/ppermute | solution.py:387
  20.4 25.7 %collective-permute-start.6 = (bf16[128,1536]{1,0:T(8,128)(2,1)S(1)}, bf16[128,1536]{1,0:T(8,128)(2,1)S(1)}, u32[]{:S(2)}, u32[]{:S(2)}) collective-permute-start(bf16[128,1536]{1,0:T(8,128)(2,1)S(1)} %get-tuple-element.53.refs_4_), channel_id=1, source_target_pairs={{0,4},{4,0},{8,12},{12,8},{16,20},{20,16},{24,28},{28,24},{1,5},{5... | collective-permute-start | bytes 1179656 | tf_op jit(solution)/shard_map/ppermute | solution.py:387
  46.0 12.4 %collective-permute-start.36 = (bf16[128,1536]{1,0:T(8,128)(2,1)S(1)}, bf16[128,1536]{1,0:T(8,128)(2,1)S(1)}, u32[]{:S(2)}, u32[]{:S(2)}) collective-permute-start(bf16[128,1536]{1,0:T(8,128)(2,1)S(1)} %collective-permute-done.31.refs_5_), channel_id=1, source_target_pairs={{0,4},{4,0},{8,12},{12,8},{16,20},{20,16},{24,28},{28,24},{1,5},{5... | collective-permute-start | bytes 1179656 | tf_op jit(solution)/shard_map/ppermute | solution.py:387
  46.1 13.6 %collective-permute-start.37 = (bf16[128,1536]{1,0:T(8,128)(2,1)S(1)}, bf16[128,1536]{1,0:T(8,128)(2,1)S(1)}, u32[]{:S(2)}, u32[]{:S(2)}) collective-permute-start(bf16[128,1536]{1,0:T(8,128)(2,1)S(1)} %collective-permute-done.32.refs_6_), channel_id=1, source_target_pairs={{0,4},{4,0},{8,12},{12,8},{16,20},{20,16},{24,28},{28,24},{1,5},{5... | collective-permute-start | bytes 1179656 | tf_op jit(solution)/shard_map/ppermute | solution.py:387
  53.5 26.7 %collective-permute-start = (bf16[392,1024]{1,0:T(8,128)(2,1)S(1)}, bf16[392,1024]{1,0:T(8,128)(2,1)}, u32[]{:S(2)}, u32[]{:S(2)}) collective-permute-start(bf16[392,1024]{1,0:T(8,128)(2,1)S(1)} %copy-done.4), channel_id=1, source_target_pairs={{0,1},{1,0},{2,3},{3,2},{4,5},{5,4},{6,7},{7,6},{8,9},{9,8},{10,11... | collective-permute-start | bytes 2408456 | tf_op jit(solution)/shard_map/ppermute | solution.py:391
  54.8 35.5 %collective-permute-start.1 = (bf16[392,1024]{1,0:T(8,128)(2,1)S(1)}, bf16[392,1024]{1,0:T(8,128)(2,1)}, u32[]{:S(2)}, u32[]{:S(2)}) collective-permute-start(bf16[392,1024]{1,0:T(8,128)(2,1)S(1)} %copy-done.5), channel_id=1, source_target_pairs={{0,1},{1,0},{2,3},{3,2},{4,5},{5,4},{6,7},{7,6},{8,9},{9,8},{10,11... | collective-permute-start | bytes 2408456 | tf_op jit(solution)/shard_map/ppermute | solution.py:391
  57.0 12.4 %collective-permute-start.22 = (bf16[128,1536]{1,0:T(8,128)(2,1)}, bf16[128,1536]{1,0:T(8,128)(2,1)}, u32[]{:S(2)}, u32[]{:S(2)}) collective-permute-start(bf16[128,1536]{1,0:T(8,128)(2,1)} %collective-permute-done.21.refs_4_), channel_id=1, source_target_pairs={{0,8},{4,12},{8,0},{12,4},{16,24},{20,28},{24,16},{28,20},{1,9},{5... | collective-permute-start | bytes 1179656 | tf_op jit(solution)/shard_map/ppermute | solution.py:387
  60.5 15.4 %collective-permute-start.12 = (bf16[128,1536]{1,0:T(8,128)(2,1)}, bf16[128,1536]{1,0:T(8,128)(2,1)}, u32[]{:S(2)}, u32[]{:S(2)}) collective-permute-start(bf16[128,1536]{1,0:T(8,128)(2,1)} %collective-permute-done.11.refs_4_), channel_id=1, source_target_pairs={{0,8},{4,12},{8,0},{12,4},{16,24},{20,28},{24,16},{28,20},{1,9},{5... | collective-permute-start | bytes 1179656 | tf_op jit(solution)/shard_map/ppermute | solution.py:387
  70.6 28.1 %collective-permute-start.26 = (bf16[128,1536]{1,0:T(8,128)(2,1)}, bf16[128,1536]{1,0:T(8,128)(2,1)}, u32[]{:S(2)}, u32[]{:S(2)}) collective-permute-start(bf16[128,1536]{1,0:T(8,128)(2,1)} %collective-permute-done.21.refs_4_), channel_id=1, source_target_pairs={{0,4},{4,0},{8,12},{12,8},{16,20},{20,16},{24,28},{28,24},{1,5},{5... | collective-permute-start | bytes 1179656 | tf_op jit(solution)/shard_map/ppermute | solution.py:387
  75.8 23.9 %collective-permute-start.16 = (bf16[128,1536]{1,0:T(8,128)(2,1)}, bf16[128,1536]{1,0:T(8,128)(2,1)}, u32[]{:S(2)}, u32[]{:S(2)}) collective-permute-start(bf16[128,1536]{1,0:T(8,128)(2,1)} %collective-permute-done.11.refs_4_), channel_id=1, source_target_pairs={{0,4},{4,0},{8,12},{12,8},{16,20},{20,16},{24,28},{28,24},{1,5},{5... | collective-permute-start | bytes 1179656 | tf_op jit(solution)/shard_map/ppermute | solution.py:387
  79.6 20.1 %collective-permute-start.24 = (bf16[64,1536]{1,0:T(8,128)(2,1)S(1)}, bf16[64,1536]{1,0:T(8,128)(2,1)S(1)}, u32[]{:S(2)}, u32[]{:S(2)}) collective-permute-start(bf16[64,1536]{1,0:T(8,128)(2,1)S(1)} %slice.309), channel_id=1, source_target_pairs={{0,16},{4,20},{8,24},{12,28},{16,0},{20,4},{24,8},{28,12},{1,17},{... | collective-permute-start | bytes 589832 | tf_op jit(solution)/shard_map/ppermute | solution.py:387
  80.2 20.1 %collective-permute-start.25 = (bf16[64,1536]{1,0:T(8,128)(2,1)S(1)}, bf16[64,1536]{1,0:T(8,128)(2,1)S(1)}, u32[]{:S(2)}, u32[]{:S(2)}) collective-permute-start(bf16[64,1536]{1,0:T(8,128)(2,1)S(1)} %slice.310), channel_id=1, source_target_pairs={{0,8},{4,12},{8,0},{12,4},{16,24},{20,28},{24,16},{28,20},{1,9},{5... | collective-permute-start | bytes 589832 | tf_op jit(solution)/shard_map/ppermute | solution.py:387
  98.7 24.8 %collective-permute-start.15 = (bf16[64,1536]{1,0:T(8,128)(2,1)S(1)}, bf16[64,1536]{1,0:T(8,128)(2,1)S(1)}, u32[]{:S(2)}, u32[]{:S(2)}) collective-permute-start(bf16[64,1536]{1,0:T(8,128)(2,1)S(1)} %slice.308), channel_id=1, source_target_pairs={{0,8},{4,12},{8,0},{12,4},{16,24},{20,28},{24,16},{28,20},{1,9},{5... | collective-permute-start | bytes 589832 | tf_op jit(solution)/shard_map/ppermute | solution.py:387
  99.7 24.4 %collective-permute-start.27 = (bf16[128,1536]{1,0:T(8,128)(2,1)}, bf16[128,1536]{1,0:T(8,128)(2,1)S(1)}, u32[]{:S(2)}, u32[]{:S(2)}) collective-permute-start(bf16[128,1536]{1,0:T(8,128)(2,1)} %collective-permute-done.22.refs_5_), channel_id=1, source_target_pairs={{0,4},{4,0},{8,12},{12,8},{16,20},{20,16},{24,28},{28,24},{1,5},{5... | collective-permute-start | bytes 1179656 | tf_op jit(solution)/shard_map/ppermute | solution.py:387
  99.7 24.8 %collective-permute-start.28 = (bf16[128,1536]{1,0:T(8,128)(2,1)}, bf16[128,1536]{1,0:T(8,128)(2,1)S(1)}, u32[]{:S(2)}, u32[]{:S(2)}) collective-permute-start(bf16[128,1536]{1,0:T(8,128)(2,1)} %collective-permute-done.23.refs_6_), channel_id=1, source_target_pairs={{0,4},{4,0},{8,12},{12,8},{16,20},{20,16},{24,28},{28,24},{1,5},{5... | collective-permute-start | bytes 1179656 | tf_op jit(solution)/shard_map/ppermute | solution.py:387
  100.3 23.4 %collective-permute-start.29 = (bf16[64,1536]{1,0:T(8,128)(2,1)S(1)}, bf16[64,1536]{1,0:T(8,128)(2,1)S(1)}, u32[]{:S(2)}, u32[]{:S(2)}) collective-permute-start(bf16[64,1536]{1,0:T(8,128)(2,1)S(1)} %collective-permute-done.24.refs_7_), channel_id=1, source_target_pairs={{0,4},{4,0},{8,12},{12,8},{16,20},{20,16},{24,28},{28,24},{1,5},{5... | collective-permute-start | bytes 589832 | tf_op jit(solution)/shard_map/ppermute | solution.py:387
  100.3 23.7 %collective-permute-start.30 = (bf16[64,1536]{1,0:T(8,128)(2,1)S(1)}, bf16[64,1536]{1,0:T(8,128)(2,1)S(1)}, u32[]{:S(2)}, u32[]{:S(2)}) collective-permute-start(bf16[64,1536]{1,0:T(8,128)(2,1)S(1)} %collective-permute-done.25.refs_8_), channel_id=1, source_target_pairs={{0,4},{4,0},{8,12},{12,8},{16,20},{20,16},{24,28},{28,24},{1,5},{5... | collective-permute-start | bytes 589832 | tf_op jit(solution)/shard_map/ppermute | solution.py:387
  123.5 24.3 %collective-permute-start.17 = (bf16[128,1536]{1,0:T(8,128)(2,1)}, bf16[128,1536]{1,0:T(8,128)(2,1)S(1)}, u32[]{:S(2)}, u32[]{:S(2)}) collective-permute-start(bf16[128,1536]{1,0:T(8,128)(2,1)} %collective-permute-done.12.refs_5_), channel_id=1, source_target_pairs={{0,4},{4,0},{8,12},{12,8},{16,20},{20,16},{24,28},{28,24},{1,5},{5... | collective-permute-start | bytes 1179656 | tf_op jit(solution)/shard_map/ppermute | solution.py:387
  123.6 24.6 %collective-permute-start.18 = (bf16[128,1536]{1,0:T(8,128)(2,1)}, bf16[128,1536]{1,0:T(8,128)(2,1)S(1)}, u32[]{:S(2)}, u32[]{:S(2)}) collective-permute-start(bf16[128,1536]{1,0:T(8,128)(2,1)} %collective-permute-done.13.refs_6_), channel_id=1, source_target_pairs={{0,4},{4,0},{8,12},{12,8},{16,20},{20,16},{24,28},{28,24},{1,5},{5... | collective-permute-start | bytes 1179656 | tf_op jit(solution)/shard_map/ppermute | solution.py:387
  124.1 70.6 %collective-permute-start.42 = (bf16[512,1536]{1,0:T(8,128)(2,1)}, bf16[512,1536]{1,0:T(8,128)(2,1)}, u32[]{:S(2)}, u32[]{:S(2)}) collective-permute-start(bf16[512,1536]{1,0:T(8,128)(2,1)} %get-tuple-element.72), channel_id=1, source_target_pairs={{0,4},{4,0},{8,12},{12,8},{16,20},{20,16},{24,28},{28,24},{1,5},{5... | collective-permute-start | bytes 4718600 | tf_op jit(solution)/shard_map/ppermute | solution.py:387
  124.1 23.0 %collective-permute-start.19 = (bf16[64,1536]{1,0:T(8,128)(2,1)S(1)}, bf16[64,1536]{1,0:T(8,128)(2,1)S(1)}, u32[]{:S(2)}, u32[]{:S(2)}) collective-permute-start(bf16[64,1536]{1,0:T(8,128)(2,1)S(1)} %collective-permute-done.14.refs_7_), channel_id=1, source_target_pairs={{0,4},{4,0},{8,12},{12,8},{16,20},{20,16},{24,28},{28,24},{1,5},{5... | collective-permute-start | bytes 589832 | tf_op jit(solution)/shard_map/ppermute | solution.py:387
  124.6 23.1 %collective-permute-start.20 = (bf16[64,1536]{1,0:T(8,128)(2,1)S(1)}, bf16[64,1536]{1,0:T(8,128)(2,1)S(1)}, u32[]{:S(2)}, u32[]{:S(2)}) collective-permute-start(bf16[64,1536]{1,0:T(8,128)(2,1)S(1)} %collective-permute-done.15.refs_8_), channel_id=1, source_target_pairs={{0,4},{4,0},{8,12},{12,8},{16,20},{20,16},{24,28},{28,24},{1,5},{5... | collective-permute-start | bytes 589832 | tf_op jit(solution)/shard_map/ppermute | solution.py:387
  147.2 24.1 %collective-permute-start.7 = (bf16[128,1536]{1,0:T(8,128)(2,1)S(1)}, bf16[128,1536]{1,0:T(8,128)(2,1)S(1)}, u32[]{:S(2)}, u32[]{:S(2)}) collective-permute-start(bf16[128,1536]{1,0:T(8,128)(2,1)S(1)} %copy-done.20), channel_id=1, source_target_pairs={{0,4},{4,0},{8,12},{12,8},{16,20},{20,16},{24,28},{28,24},{1,5},{5... | collective-permute-start | bytes 1179656 | tf_op jit(solution)/shard_map/ppermute | solution.py:387
  147.7 23.6 %collective-permute-start.8 = (bf16[128,1536]{1,0:T(8,128)(2,1)S(1)}, bf16[128,1536]{1,0:T(8,128)(2,1)S(1)}, u32[]{:S(2)}, u32[]{:S(2)}) collective-permute-start(bf16[128,1536]{1,0:T(8,128)(2,1)S(1)} %collective-permute-done.3.refs_6_), channel_id=1, source_target_pairs={{0,4},{4,0},{8,12},{12,8},{16,20},{20,16},{24,28},{28,24},{1,5},{5... | collective-permute-start | bytes 1179656 | tf_op jit(solution)/shard_map/ppermute | solution.py:387
  147.8 23.0 %collective-permute-start.10 = (bf16[64,1536]{1,0:T(8,128)(2,1)S(1)}, bf16[64,1536]{1,0:T(8,128)(2,1)S(1)}, u32[]{:S(2)}, u32[]{:S(2)}) collective-permute-start(bf16[64,1536]{1,0:T(8,128)(2,1)S(1)} %collective-permute-done.5.refs_8_), channel_id=1, source_target_pairs={{0,4},{4,0},{8,12},{12,8},{16,20},{20,16},{24,28},{28,24},{1,5},{5... | collective-permute-start | bytes 589832 | tf_op jit(solution)/shard_map/ppermute | solution.py:387
  148.2 23.1 %collective-permute-start.9 = (bf16[64,1536]{1,0:T(8,128)(2,1)S(1)}, bf16[64,1536]{1,0:T(8,128)(2,1)S(1)}, u32[]{:S(2)}, u32[]{:S(2)}) collective-permute-start(bf16[64,1536]{1,0:T(8,128)(2,1)S(1)} %collective-permute-done.4.refs_7_), channel_id=1, source_target_pairs={{0,4},{4,0},{8,12},{12,8},{16,20},{20,16},{24,28},{28,24},{1,5},{5... | collective-permute-start | bytes 589832 | tf_op jit(solution)/shard_map/ppermute | solution.py:387
  170.8 35.6 %collective-permute-start.53 = (bf16[512,1536]{1,0:T(8,128)(2,1)}, bf16[512,1536]{1,0:T(8,128)(2,1)S(1)}, u32[]{:S(2)}, u32[]{:S(2)}) collective-permute-start(bf16[512,1536]{1,0:T(8,128)(2,1)} %get-tuple-element.76), channel_id=1, source_target_pairs={{0,4},{4,0},{8,12},{12,8},{16,20},{20,16},{24,28},{28,24},{1,5},{5... | collective-permute-start | bytes 4718600 | tf_op jit(solution)/shard_map/ppermute | solution.py:387
  194.1 13.7 %collective-permute-start.59 = (bf16[512,1536]{1,0:T(8,128)(2,1)}, bf16[512,1536]{1,0:T(8,128)(2,1)S(1)}, u32[]{:S(2)}, u32[]{:S(2)}) collective-permute-start(bf16[512,1536]{1,0:T(8,128)(2,1)} %get-tuple-element.78), channel_id=1, source_target_pairs={{0,4},{4,0},{8,12},{12,8},{16,20},{20,16},{24,28},{28,24},{1,5},{5... | collective-permute-start | bytes 4718600 | tf_op jit(solution)/shard_map/ppermute | solution.py:387
  194.2 14.4 %collective-permute-start.47 = (bf16[512,1536]{1,0:T(8,128)(2,1)}, bf16[512,1536]{1,0:T(8,128)(2,1)S(1)}, u32[]{:S(2)}, u32[]{:S(2)}) collective-permute-start(bf16[512,1536]{1,0:T(8,128)(2,1)} %get-tuple-element.74), channel_id=1, source_target_pairs={{0,4},{4,0},{8,12},{12,8},{16,20},{20,16},{24,28},{28,24},{1,5},{5... | collective-permute-start | bytes 4718600 | tf_op jit(solution)/shard_map/ppermute | solution.py:387
  202.8 55.1 %collective-permute-start.41 = (bf16[416,1024]{1,0:T(8,128)(2,1)S(1)}, bf16[416,1024]{1,0:T(8,128)(2,1)S(1)}, u32[]{:S(2)}, u32[]{:S(2)}) collective-permute-start(bf16[416,1024]{1,0:T(8,128)(2,1)S(1)} %copy-done.49), channel_id=1, source_target_pairs={{0,1},{1,0},{2,3},{3,2},{4,5},{5,4},{6,7},{7,6},{8,9},{9,8},{10,11... | collective-permute-start | bytes 2555912 | tf_op jit(solution)/shard_map/ppermute | solution.py:391
  205.4 77.1 %collective-permute-start.44 = (bf16[128,1536]{1,0:T(8,128)(2,1)S(1)}, bf16[128,1536]{1,0:T(8,128)(2,1)S(1)}, u32[]{:S(2)}, u32[]{:S(2)}) collective-permute-start(bf16[128,1536]{1,0:T(8,128)(2,1)S(1)} %get-tuple-element.121), channel_id=1, source_target_pairs={{0,8},{4,12},{8,0},{12,4},{16,24},{20,28},{24,16},{28,20},{1,9},{5... | collective-permute-start | bytes 1179656 | tf_op jit(solution)/shard_map/ppermute | solution.py:387
  207.8 13.9 %collective-permute-start.56 = (bf16[64,1536]{1,0:T(8,128)(2,1)S(1)}, bf16[64,1536]{1,0:T(8,128)(2,1)S(1)}, u32[]{:S(2)}, u32[]{:S(2)}) collective-permute-start(bf16[64,1536]{1,0:T(8,128)(2,1)S(1)} %get-tuple-element.126), channel_id=1, source_target_pairs={{0,8},{4,12},{8,0},{12,4},{16,24},{20,28},{24,16},{28,20},{1,9},{5... | collective-permute-start | bytes 589832 | tf_op jit(solution)/shard_map/ppermute | solution.py:387
  208.7 14.1 %collective-permute-start.60 = (bf16[64,1536]{1,0:T(8,128)(2,1)S(1)}, bf16[64,1536]{1,0:T(8,128)(2,1)S(1)}, u32[]{:S(2)}, u32[]{:S(2)}) collective-permute-start(bf16[64,1536]{1,0:T(8,128)(2,1)S(1)} %get-tuple-element.127), channel_id=1, source_target_pairs={{0,16},{4,20},{8,24},{12,28},{16,0},{20,4},{24,8},{28,12},{1,17},{... | collective-permute-start | bytes 589832 | tf_op jit(solution)/shard_map/ppermute | solution.py:387
  225.9 13.2 %collective-permute-start.55 = (bf16[128,1536]{1,0:T(8,128)(2,1)S(1)}, bf16[128,1536]{1,0:T(8,128)(2,1)S(1)}, u32[]{:S(2)}, u32[]{:S(2)}) collective-permute-start(bf16[128,1536]{1,0:T(8,128)(2,1)S(1)} %get-tuple-element.117), channel_id=1, source_target_pairs={{0,8},{4,12},{8,0},{12,4},{16,24},{20,28},{24,16},{28,20},{1,9},{5... | collective-permute-start | bytes 1179656 | tf_op jit(solution)/shard_map/ppermute | solution.py:387
  230.7 27.7 %collective-permute-start.61 = (bf16[128,1536]{1,0:T(8,128)(2,1)S(1)}, bf16[128,1536]{1,0:T(8,128)(2,1)S(1)}, u32[]{:S(2)}, u32[]{:S(2)}) collective-permute-start(bf16[128,1536]{1,0:T(8,128)(2,1)S(1)} %get-tuple-element.119), channel_id=1, source_target_pairs={{0,8},{4,12},{8,0},{12,4},{16,24},{20,28},{24,16},{28,20},{1,9},{5... | collective-permute-start | bytes 1179656 | tf_op jit(solution)/shard_map/ppermute | solution.py:387
  239.2 14.1 %collective-permute-start.49 = (bf16[128,1536]{1,0:T(8,128)(2,1)S(1)}, bf16[128,1536]{1,0:T(8,128)(2,1)S(1)}, u32[]{:S(2)}, u32[]{:S(2)}) collective-permute-start(bf16[128,1536]{1,0:T(8,128)(2,1)S(1)} %get-tuple-element.123), channel_id=1, source_target_pairs={{0,8},{4,12},{8,0},{12,4},{16,24},{20,28},{24,16},{28,20},{1,9},{5... | collective-permute-start | bytes 1179656 | tf_op jit(solution)/shard_map/ppermute | solution.py:387
  240.5 13.8 %collective-permute-start.51 = (bf16[128,1536]{1,0:T(8,128)(2,1)S(1)}, bf16[128,1536]{1,0:T(8,128)(2,1)S(1)}, u32[]{:S(2)}, u32[]{:S(2)}) collective-permute-start(bf16[128,1536]{1,0:T(8,128)(2,1)S(1)} %get-tuple-element.124), channel_id=1, source_target_pairs={{0,16},{4,20},{8,24},{12,28},{16,0},{20,4},{24,8},{28,12},{1,17},{... | collective-permute-start | bytes 1179656 | tf_op jit(solution)/shard_map/ppermute | solution.py:387
  253.3 12.1 %collective-permute-start.63 = (bf16[128,1536]{1,0:T(8,128)(2,1)S(1)}, bf16[128,1536]{1,0:T(8,128)(2,1)S(1)}, u32[]{:S(2)}, u32[]{:S(2)}) collective-permute-start(bf16[128,1536]{1,0:T(8,128)(2,1)S(1)} %get-tuple-element.120), channel_id=1, source_target_pairs={{0,16},{4,20},{8,24},{12,28},{16,0},{20,4},{24,8},{28,12},{1,17},{... | collective-permute-start | bytes 1179656 | tf_op jit(solution)/shard_map/ppermute | solution.py:387
  254.2 27.4 %collective-permute-start.58 = (bf16[128,1536]{1,0:T(8,128)(2,1)S(1)}, bf16[128,1536]{1,0:T(8,128)(2,1)S(1)}, u32[]{:S(2)}, u32[]{:S(2)}) collective-permute-start(bf16[128,1536]{1,0:T(8,128)(2,1)S(1)} %add_convert_fusion.3), channel_id=1, source_target_pairs={{0,2},{1,3},{2,0},{3,1},{4,6},{5,7},{6,4},{7,5},{8,10},{9,11},{10,... | collective-permute-start | bytes 1179656 | tf_op jit(solution)/shard_map/ppermute | solution.py:391
  257.9 24.6 %collective-permute-start.46 = (bf16[128,1536]{1,0:T(8,128)(2,1)S(1)}, bf16[128,1536]{1,0:T(8,128)(2,1)S(1)}, u32[]{:S(2)}, u32[]{:S(2)}) collective-permute-start(bf16[128,1536]{1,0:T(8,128)(2,1)S(1)} %get-tuple-element.122), channel_id=1, source_target_pairs={{0,16},{4,20},{8,24},{12,28},{16,0},{20,4},{24,8},{28,12},{1,17},{... | collective-permute-start | bytes 1179656 | tf_op jit(solution)/shard_map/ppermute | solution.py:387
  258.5 31.4 %collective-permute-start.52 = (bf16[128,1536]{1,0:T(8,128)(2,1)S(1)}, bf16[128,1536]{1,0:T(8,128)(2,1)S(1)}, u32[]{:S(2)}, u32[]{:S(2)}) collective-permute-start(bf16[128,1536]{1,0:T(8,128)(2,1)S(1)} %add_convert_fusion.7), channel_id=1, source_target_pairs={{0,2},{1,3},{2,0},{3,1},{4,6},{5,7},{6,4},{7,5},{8,10},{9,11},{10,... | collective-permute-start | bytes 1179656 | tf_op jit(solution)/shard_map/ppermute | solution.py:391
  265.3 36.9 %collective-permute-start.40 = (bf16[416,1024]{1,0:T(8,128)(2,1)}, bf16[416,1024]{1,0:T(8,128)(2,1)}, u32[]{:S(2)}, u32[]{:S(2)}) collective-permute-start(bf16[416,1024]{1,0:T(8,128)(2,1)} %get-tuple-element.62), channel_id=1, source_target_pairs={{0,1},{1,0},{2,3},{3,2},{4,5},{5,4},{6,7},{7,6},{8,9},{9,8},{10,11... | collective-permute-start | bytes 2555912 | tf_op jit(solution)/shard_map/ppermute | solution.py:391
  296.0 14.4 %all-to-all-start = ((f32[32,16,128]{2,1,0:T(8,128)}), f32[32,16,128]{2,1,0:T(8,128)S(1)}, u32[]{:S(2)}, u32[]{:S(2)}) async-start(f32[32,16,128]{2,1,0:T(8,128)} %broadcast_in_dim.15), calls=%async_computation | async-start | bytes 524288 | tf_op jit(solution)/shard_map/all_to_all | solution.py:442
  (69 other events, 844.0 us)
